TPU v7x, 32 devices: a whole 2x2x4 slice. The times are simulated.
32 devices in a mesh: sub: 8 (over z, x), coarse: 4 (over y, core).
Axes of the slice: x: 2, y: 2, z: 4, core: 2. Of those that a mesh axis runs over, the one named last changes fastest.
Arguments:
- loads: float32 [8, 4, 16, 16, 128], P('sub', 'coarse'), may hold values from -18 to 18
- mode_x: float32 [8, 4, 16, 16], P('sub', 'coarse'), may hold values from -1 to 2
- mode_y: float32 [8, 4, 16, 16], P('sub', 'coarse'), may hold values from -1 to 2
- mode_z: float32 [8, 4, 128, 128], P('sub', 'coarse'), may hold values from -1 to 2
- eigen: float32 [8, 4, 160], P('sub', 'coarse'), may hold values from 0.1 to 2
- classes: int32 [8, 4, 4, 4, 32], P('sub', 'coarse'), may hold values from 0 to 15
- coefficients: float32 [16], replicated, may hold values from 0.25 to 4
- partner: int32 [8, 4, 4, 2], P('sub', 'coarse'), may hold values from 0 to 7, as said below
- rows: int32 [8, 4, 4, 2048], P('sub', 'coarse'), may hold values from 0 to 32767, as said below
- corner_id: int32 [8, 4, 8], P('sub', 'coarse'), may hold values from 0 to 31, as said below
- corner_row: int32 [8, 4, 8], P('sub', 'coarse'), may hold values from 0 to 32767, as said below
- coarse_inverse: float32 [32, 32], P('coarse'), may hold values from -1 to 3, as said below
Outputs:
- multipliers: float32 [8, 4, 4, 2048], P('sub', 'coarse')
- residual: float32 [8, 4, 4, 2048], P('sub', 'coarse')
Inputs may be any that keep to these rules, and one draw needn't show every extreme that they name: partner[i, j, c] differs from (i, j) by one in exactly one index, cyclically; partner[partner[i, j, c], c] = (i, j); the 4 partners of one subdomain are its four cyclic neighbours. `rows`: within one subdomain all 4 x 2048 entries are distinct. `corner_id`: within one subdomain the 8 entries are distinct. `corner_row`: within one subdomain the 8 entries are distinct. `coarse_inverse`: symmetric.
All inputs are finite; a program needn't handle non-finite values.
Results may differ from a plain program's by a relative error of at most 0.0003.
Values sent between devices are 32-bit elements; how exact they have to be, the bound alone decides.
A program may use at most 64 MiB of HBM per device.

v0:
```python
import jax
import jax.numpy as jnp
from jax import lax
from jax.sharding import PartitionSpec as P

ITERS = 2


def padded_2(x, sides, width):
    for axis, dim in sides:
        size, length = (lax.axis_size(axis), x.shape[dim])
        up = [(i, (i + 1) % size) for i in range(size)]
        down = [(j, i) for i, j in up]
        last = lax.slice_in_dim(x, length - width, length, axis=dim)
        leading = lax.slice_in_dim(x, 0, width, axis=dim)
        before = lax.ppermute(last, axis, up)
        after = lax.ppermute(leading, axis, down)
        x = jnp.concatenate([before, x, after], axis=dim)
    return x


def on_device(
    loads,
    mode_x,
    mode_y,
    mode_z,
    eigen,
    classes,
    coefficients,
    partner,
    rows,
    corner_id,
    corner_row,
    coarse_inverse,
):
    side_x = mode_x[0, 0]
    side_y = mode_y[0, 0]
    side_z = mode_z[0, 0]
    size_x = side_x.shape[0]
    size_y = side_y.shape[0]
    size_z = side_z.shape[0]
    plane = size_x * size_y
    side_pair = (side_x[:, None, :, None] * side_y[None, :, None, :]).reshape(plane, plane)
    spectrum = eigen[0, 0]
    lam_inv = 1.0 / (
        spectrum[:size_x][:, None, None]
        + spectrum[size_x : size_x + size_y][None, :, None]
        + spectrum[size_x + size_y :][None, None, :]
    )
    lam_inv = lam_inv.reshape(plane, size_z)
    class_ids = jnp.arange(coefficients.shape[0], dtype=jnp.int32)
    class_table = class_ids[:, None, None, None] == classes[0, 0][None]
    coef_elem = jnp.sum(jnp.where(class_table, coefficients[:, None, None, None], 0.0), axis=0)
    coef_node = jnp.repeat(jnp.repeat(jnp.repeat(coef_elem, 4, axis=0), 4, axis=1), 4, axis=2)
    inv_root = (1.0 / jnp.sqrt(coef_node)).reshape(plane, size_z)
    sub_count = lax.axis_size("sub")
    column_count = lax.axis_size("coarse")
    myself = lax.axis_index("sub")
    my_column = lax.axis_index("coarse")
    matched = partner[0, 0]
    matched_sub = matched[:, 0]
    matched_col = matched[:, 1]
    sign = jnp.where(
        myself * column_count + my_column < matched_sub * column_count + matched_col, 1.0, -1.0
    ).astype(jnp.float32)[:, None]
    local_rows = rows[0, 0]
    flat_rows = local_rows.reshape(-1)
    corner_nodes = corner_row[0, 0]
    corner_ids = corner_id[0, 0]
    total_corners = coarse_inverse.shape[1]
    nodes = plane * size_z

    def solve(field):
        values = field.reshape(plane, size_z) * inv_root
        values = jnp.einsum("pa,pz->az", side_pair, values, precision=lax.Precision.HIGHEST)
        values = jnp.einsum("xp,pc->xc", values, side_z, precision=lax.Precision.HIGHEST)
        values = values * lam_inv
        values = jnp.einsum("ap,pz->az", side_pair, values, precision=lax.Precision.HIGHEST)
        values = jnp.einsum("xp,cp->xc", values, side_z, precision=lax.Precision.HIGHEST)
        return (values * inv_root).reshape(-1)

    same_column = matched_col == my_column
    same_sub = matched_sub == myself
    prev_sub = same_column & (matched_sub == (myself - 1) % sub_count)
    next_col = same_sub & (matched_col == (my_column + 1) % column_count)
    prev_col = same_sub & (matched_col == (my_column - 1) % column_count)

    def partner_of(values):
        padded = padded_2(values[None, None], (("sub", 0), ("coarse", 1)), 1)
        result = jnp.where(prev_sub[:, None], padded[0, 1], padded[2, 1])
        result = jnp.where(prev_col[:, None], padded[1, 0], result)
        return jnp.where(next_col[:, None], padded[1, 2], result)

    load_field = solve(loads[0, 0].reshape(-1))
    load_values = load_field[local_rows]
    a_rows = coef_node.reshape(-1)[local_rows]
    width = load_values.shape[1]
    far_values = partner_of(jnp.concatenate([load_values, a_rows], axis=1))
    rhs = sign * (load_values - far_values[:, :width])
    a_far = far_values[:, width:]
    weight = a_rows * a_far / (a_rows + a_far)
    multipliers = jnp.zeros_like(rhs)
    residual = rhs

    def precond_dot(resid, pre):
        return lax.psum(jnp.sum(resid * pre), ("sub", "coarse"))

    precond = weight * residual
    direction = precond
    rz_now = precond_dot(residual, precond)
    for step in range(ITERS):
        source = jnp.zeros((nodes,), jnp.float32).at[flat_rows].set((sign * direction).reshape(-1))
        local = solve(source)
        partial_corner = local[corner_nodes]
        corner_table = corner_ids[:, None] == jnp.arange(total_corners, dtype=jnp.int32)[None, :]
        apply_term = jnp.sum(jnp.where(corner_table, partial_corner[:, None], 0.0), axis=0)
        column = lax.psum(apply_term, "sub")
        total = lax.psum(column, "coarse")
        owned = jnp.dot(coarse_inverse, total, precision=lax.Precision.HIGHEST)
        coarse_sol = lax.all_gather(owned, "coarse", axis=0, tiled=True)
        extra = jnp.zeros((nodes,), jnp.float32).at[corner_nodes].set(coarse_sol[corner_ids])
        apply_values = (local + solve(extra))[local_rows]
        image = sign * (apply_values - partner_of(apply_values))
        alpha = rz_now / lax.psum(jnp.sum(direction * image), ("sub", "coarse"))
        multipliers = multipliers + alpha * direction
        residual = residual - alpha * image
        if step + 1 < ITERS:
            precond = weight * residual
            rz_next = precond_dot(residual, precond)
            direction = precond + rz_next / rz_now * direction
            rz_now = rz_next
    return (multipliers[None, None], residual[None, None])


def solution(mesh):
    placed = (
        P("sub", "coarse", None, None, None),
        P("sub", "coarse", None, None),
        P("sub", "coarse", None, None),
        P("sub", "coarse", None, None),
        P("sub", "coarse", None),
        P("sub", "coarse", None, None, None),
        P(),
        P("sub", "coarse", None, None),
        P("sub", "coarse", None, None),
        P("sub", "coarse", None),
        P("sub", "coarse", None),
        P("coarse", None),
    )
    return jax.shard_map(
        on_device,
        mesh=mesh,
        in_specs=placed,
        out_specs=(P("sub", "coarse", None, None), P("sub", "coarse", None, None)),
        check_vma=False,
    )
```

profile of v0, /device:TPU:0, one launch (start us, length us, event | category | flops | bytes accessed | tf_op | source)
XLA Modules:
  0.0 503.9 jit_solution(13656839619324459873)
XLA Ops:
  3.1 2.6 broadcast_in_dim.155
  5.7 4.9 reshape_reshape.3
  10.6 45.5 %gather_fusion.1 = f32[8192]{0:T(1024)S(1)} fusion(f32[32768]{0:T(1024)S(1)} %reshape_reshape.3, s32[8192]{0:T(1024)S(1)} %broadcast_clamp_fusion), kind=kCustom, calls=%fused_computation.1 | custom fusion | bytes 98304 | tf_op jit(solution)/shard_map/gather | solution.py:96
  57.0 1.6 broadcast_multiply_fusion
  58.6 2.5 mul.201
  63.3 45.5 %gather_fusion = f32[8192]{0:T(1024)S(1)} fusion(f32[32768]{0:T(1024)S(1)} %fusion.6, s32[8192]{0:T(1024)S(1)} %broadcast_clamp_fusion), kind=kCustom, calls=%fused_computation | custom fusion | bytes 98304 | tf_op jit(solution)/shard_map/gather | solution.py:95
  109.0 6.0 %collective-permute-start.1 = (f32[1,1,4,4096]{3,2,1,0:T(4,128)S(1)}, f32[1,1,4,4096]{3,2,1,0:T(4,128)S(1)}, u32[]{:S(2)}, u32[]{:S(2)}) collective-permute-start(f32[1,1,4,4096]{3,2,1,0:T(4,128)S(1)} %maximum_bitcast_fusion), channel_id=1, source_target_pairs={{4,0},{8,4},{12,8},{16,12},{20,16},{24,20},{28,24},{0,28},{5,1},{9... | collective-permute-start | bytes 196616 | tf_op jit(solution)/shard_map/ppermute | solution.py:17
  116.9 5.1 %collective-permute-done = f32[1,1,4,4096]{3,2,1,0:T(4,128)S(1)} collective-permute-done((f32[1,1,4,4096]{3,2,1,0:T(4,128)S(1)}, f32[1,1,4,4096]{3,2,1,0:T(4,128)S(1)}, u32[]{:S(2)}, u32[]{:S(2)}) %collective-permute-start) | collective-permute-done | bytes 65568 | tf_op jit(solution)/shard_map/ppermute | solution.py:16
  122.1 1.7 collective-permute-start.2
  123.8 3.6 collective-permute-done.3
  128.5 30.5 %scatter_custom_fusion = f32[32768]{0:T(1024)S(1)} fusion(s32[8192]{0:T(1024)S(1)} %bitcast.219, f32[8192]{0:T(1024)S(1)} %bitcast.222, f32[]{:T(128)} %constant.50.clone.1), kind=kCustom, calls=%fused_computation.76 | custom fusion | bytes 131076 | tf_op jit(solution)/shard_map/scatter | solution.py:112
  161.2 17.1 %psum.57 = f32[32]{0:T(128)S(1)} all-reduce(f32[32]{0:T(128)S(1)} %select_reduce_fusion.2), channel_id=1, replica_groups=mesh['sub'=8,'coarse'=4] {'sub'}, use_global_device_ids=true, to_apply=%region_5.6 | all-reduce | flops 32 | bytes 256 | tf_op jit(solution)/shard_map/psum | solution.py:117
  178.4 5.6 %psum.58 = f32[32]{0:T(128)S(1)} all-reduce(f32[32]{0:T(128)S(1)} %psum.57), channel_id=1, replica_groups=mesh['sub'=8,'coarse'=4] {'coarse'}, use_global_device_ids=true, to_apply=%region_6.7 | all-reduce | flops 32 | bytes 256 | tf_op jit(solution)/shard_map/psum | solution.py:118
  184.4 6.8 %all-reduce = f32[32]{0:T(128)S(1)} all-reduce(f32[32]{0:T(128)S(1)} %dynamic-update-slice), channel_id=1, replica_groups=mesh['sub'=8,'coarse'=4] {'coarse'}, use_global_device_ids=true, to_apply=%add | all-reduce | flops 32 | bytes 256
  194.2 45.5 %gather_fusion.4 = f32[8192]{0:T(1024)S(1)} fusion(f32[32768]{0:T(1024)S(1)} %fusion.4, s32[8192]{0:T(1024)S(1)} %broadcast_clamp_fusion), kind=kCustom, calls=%fused_computation.4 | custom fusion | bytes 98304 | tf_op jit(solution)/shard_map/gather | solution.py:122
  239.8 2.1 collective-permute-start.4
  241.8 2.7 collective-permute-start.5
  244.6 1.9 collective-permute-done.4
  246.5 1.7 collective-permute-start.6
  248.3 2.3 collective-permute-done.7
  251.4 39.7 %all-reduce.2 = (f32[]{:T(128)}, f32[]{:T(128)}) all-reduce(f32[]{:T(128)} %get-tuple-element.3, f32[]{:T(128)} %get-tuple-element.2), channel_id=1, replica_groups=mesh['sub'=8,'coarse'=4] {'sub','coarse'}, use_global_device_ids=true, to_apply=%region_2.3 | all-reduce | flops 2 | bytes 16 | tf_op jit(solution)/shard_map/psum | solution.py:106
  292.9 41.7 %psum.60 = f32[]{:T(128)} all-reduce(f32[]{:T(128)} %get-tuple-element.8), channel_id=1, replica_groups=mesh['sub'=8,'coarse'=4] {'sub','coarse'}, use_global_device_ids=true, to_apply=%region_11.12 | all-reduce | flops 1 | bytes 8 | tf_op jit(solution)/shard_map/psum | solution.py:106
  335.9 30.5 %scatter_custom_fusion.2 = f32[32768]{0:T(1024)S(1)} fusion(s32[8192]{0:T(1024)S(1)} %bitcast.220, f32[8192]{0:T(1024)S(1)} %bitcast.221, f32[]{:T(128)} %constant.50.clone.1), kind=kCustom, calls=%fused_computation.72 | custom fusion | bytes 131076 | tf_op jit(solution)/shard_map/scatter | solution.py:112
  368.7 21.1 %psum.61 = f32[32]{0:T(128)S(1)} all-reduce(f32[32]{0:T(128)S(1)} %select_reduce_fusion.1), channel_id=1, replica_groups=mesh['sub'=8,'coarse'=4] {'sub'}, use_global_device_ids=true, to_apply=%region_14.15 | all-reduce | flops 32 | bytes 256 | tf_op jit(solution)/shard_map/psum | solution.py:117
  389.8 5.6 %psum.62 = f32[32]{0:T(128)S(1)} all-reduce(f32[32]{0:T(128)S(1)} %psum.61), channel_id=1, replica_groups=mesh['sub'=8,'coarse'=4] {'coarse'}, use_global_device_ids=true, to_apply=%region_15.16 | all-reduce | flops 32 | bytes 256 | tf_op jit(solution)/shard_map/psum | solution.py:118
  395.8 6.3 %all-reduce.1 = f32[32]{0:T(128)S(1)} all-reduce(f32[32]{0:T(128)S(1)} %dynamic-update-slice.1), channel_id=1, replica_groups=mesh['sub'=8,'coarse'=4] {'coarse'}, use_global_device_ids=true, to_apply=%add.1 | all-reduce | flops 32 | bytes 256
  404.9 45.5 %gather_fusion.7 = f32[8192]{0:T(1024)S(1)} fusion(f32[32768]{0:T(1024)S(1)} %fusion.1, s32[8192]{0:T(1024)S(1)} %broadcast_clamp_fusion), kind=kCustom, calls=%fused_computation.7 | custom fusion | bytes 98304 | tf_op jit(solution)/shard_map/gather | solution.py:122
  450.6 4.7 collective-permute-start.9
  455.3 1.9 collective-permute-done.8
  457.3 1.7 collective-permute-start.10
  459.0 2.3 collective-permute-done.11
  462.0 39.9 %psum.63 = f32[]{:T(128)} all-reduce(f32[]{:T(128)} %get-tuple-element.6), channel_id=1, replica_groups=mesh['sub'=8,'coarse'=4] {'sub','coarse'}, use_global_device_ids=true, to_apply=%region_18.19 | all-reduce | flops 1 | bytes 8 | tf_op jit(solution)/shard_map/psum | solution.py:124
  (117 shorter events, 22.0 us)
Async XLA Ops:
  0.6 61.7 %copy-start = (f32[1,1,128,128]{3,2,1,0:T(8,128)S(1)}, f32[1,1,128,128]{3,2,1,0:T(8,128)}, u32[]{:S(2)}) copy-start(f32[1,1,128,128]{3,2,1,0:T(8,128)} %param.15) | copy-start | bytes 196612
  5.7 4.9 copy-start.2
  56.1 0.8 copy-start.4
  56.2 0.8 copy-start.5
  58.6 3.2 copy-start.1
  63.3 51.8 %copy-start.7 = (s32[1,1,8]{2,1,0:T(1,128)S(1)}, s32[1,1,8]{2,1,0:T(1,128)}, u32[]{:S(2)}) copy-start(s32[1,1,8]{2,1,0:T(1,128)} %param.22) | copy-start | bytes 100
  63.3 51.8 %copy-start.8 = (s32[1,1,8]{2,1,0:T(1,128)S(1)}, s32[1,1,8]{2,1,0:T(1,128)}, u32[]{:S(2)}) copy-start(s32[1,1,8]{2,1,0:T(1,128)} %param.21) | copy-start | bytes 100
  63.3 51.8 %copy-start.9 = (u32[32]{0:T(128)S(1)}, u32[32]{0:T(128)}, u32[]{:S(2)}) copy-start(u32[32]{0:T(128)} %constant.71) | copy-start | bytes 388
  63.3 53.1 %copy-start.6 = (s32[1,1,4,2]{2,3,1,0:T(2,128)S(1)}, s32[1,1,4,2]{2,3,1,0:T(2,128)}, u32[]{:S(2)}) copy-start(s32[1,1,4,2]{2,3,1,0:T(2,128)} %param.19) | copy-start | bytes 100
  108.9 75.1 %copy-start.3 = (f32[8,32]{1,0:T(8,128)S(1)}, f32[8,32]{1,0:T(8,128)}, u32[]{:S(2)}) copy-start(f32[8,32]{1,0:T(8,128)} %param.23) | copy-start | bytes 3076
  109.0 7.9 %collective-permute-start.1 = (f32[1,1,4,4096]{3,2,1,0:T(4,128)S(1)}, f32[1,1,4,4096]{3,2,1,0:T(4,128)S(1)}, u32[]{:S(2)}, u32[]{:S(2)}) collective-permute-start(f32[1,1,4,4096]{3,2,1,0:T(4,128)S(1)} %maximum_bitcast_fusion), channel_id=1, source_target_pairs={{4,0},{8,4},{12,8},{16,12},{20,16},{24,20},{28,24},{0,28},{5,1},{9... | collective-permute-start | bytes 196616 | tf_op jit(solution)/shard_map/ppermute | solution.py:17
  115.0 7.0 %collective-permute-start = (f32[1,1,4,4096]{3,2,1,0:T(4,128)S(1)}, f32[1,1,4,4096]{3,2,1,0:T(4,128)S(1)}, u32[]{:S(2)}, u32[]{:S(2)}) collective-permute-start(f32[1,1,4,4096]{3,2,1,0:T(4,128)S(1)} %maximum_bitcast_fusion), channel_id=1, source_target_pairs={{0,4},{4,8},{8,12},{12,16},{16,20},{20,24},{24,28},{28,0},{1,5},{5... | collective-permute-start | bytes 196616 | tf_op jit(solution)/shard_map/ppermute | solution.py:16
  122.0 5.4 %collective-permute-start.3 = (f32[3,1,4,4096]{3,2,1,0:T(4,128)S(1)}, f32[3,1,4,4096]{3,2,1,0:T(4,128)S(1)}, u32[]{:S(2)}, u32[]{:S(2)}) collective-permute-start(f32[3,1,4,4096]{3,2,1,0:T(4,128)S(1)} %pad_maximum_fusion), channel_id=1, source_target_pairs={{0,1},{1,2},{2,3},{3,0},{4,5},{5,6},{6,7},{7,4},{8,9},{9,10},{10,1... | collective-permute-start | bytes 589832 | tf_op jit(solution)/shard_map/ppermute | solution.py:16
  122.1 6.2 %collective-permute-start.2 = (f32[3,1,4,4096]{3,2,1,0:T(4,128)S(1)}, f32[3,1,4,4096]{3,2,1,0:T(4,128)S(1)}, u32[]{:S(2)}, u32[]{:S(2)}) collective-permute-start(f32[3,1,4,4096]{3,2,1,0:T(4,128)S(1)} %pad_maximum_fusion), channel_id=1, source_target_pairs={{1,0},{2,1},{3,2},{0,3},{5,4},{6,5},{7,6},{4,7},{9,8},{10,9},{11,1... | collective-permute-start | bytes 589832 | tf_op jit(solution)/shard_map/ppermute | solution.py:17
  239.8 6.7 %collective-permute-start.4 = (f32[1,1,4,2048]{3,2,1,0:T(4,128)S(1)}, f32[1,1,4,2048]{3,2,1,0:T(4,128)S(1)}, u32[]{:S(2)}, u32[]{:S(2)}) collective-permute-start(f32[1,1,4,2048]{3,2,1,0:T(4,128)S(1)} %broadcast_in_dim.164), channel_id=1, source_target_pairs={{0,4},{4,8},{8,12},{12,16},{16,20},{20,24},{24,28},{28,0},{1,5},{5... | collective-permute-start | bytes 98312 | tf_op jit(solution)/shard_map/ppermute | solution.py:16
  241.8 4.6 collective-permute-start.5
  246.5 4.1 collective-permute-start.7
  246.5 4.0 collective-permute-start.6
  450.5 6.7 %collective-permute-start.8 = (f32[1,1,4,2048]{3,2,1,0:T(4,128)S(1)}, f32[1,1,4,2048]{3,2,1,0:T(4,128)S(1)}, u32[]{:S(2)}, u32[]{:S(2)}) collective-permute-start(f32[1,1,4,2048]{3,2,1,0:T(4,128)S(1)} %broadcast_in_dim.168), channel_id=1, source_target_pairs={{0,4},{4,8},{8,12},{12,16},{16,20},{20,24},{24,28},{28,0},{1,5},{5... | collective-permute-start | bytes 98312 | tf_op jit(solution)/shard_map/ppermute | solution.py:16
  450.6 6.6 %collective-permute-start.9 = (f32[1,1,4,2048]{3,2,1,0:T(4,128)S(1)}, f32[1,1,4,2048]{3,2,1,0:T(4,128)S(1)}, u32[]{:S(2)}, u32[]{:S(2)}) collective-permute-start(f32[1,1,4,2048]{3,2,1,0:T(4,128)S(1)} %broadcast_in_dim.168), channel_id=1, source_target_pairs={{4,0},{8,4},{12,8},{16,12},{20,16},{24,20},{28,24},{0,28},{5,1},{9... | collective-permute-start | bytes 98312 | tf_op jit(solution)/shard_map/ppermute | solution.py:17
  457.2 4.1 collective-permute-start.11
  457.3 4.0 collective-permute-start.10
where the time goes:
time: 505 us; the launch traced here: 504 us
  local copies, waits for them, and re-layouts  261 us (52%)
  blocking collectives  184 us (36%)
  starting transfers between devices  20.9 us (4%)
  waiting for transfers between devices  18.3 us (4%)
  matrix products  7.8 us (2%)
  between operations  5.77 us (1%)
  other arithmetic  5.72 us (1%)
    gather x4, local copies, waits for them, and re-layouts, on_device(): apply_values = (local + solve(extra))[local_rows]  91.1 us
    psum x2, blocking collectives, precond_dot(): return lax.psum(jnp.sum(resid * pre), ('sub', 'coarse'))  81.4 us
    scatter x2, local copies, waits for them, and re-layouts, on_device(): jnp.zeros((nodes,), jnp.float32).at[flat_rows]  61 us
    gather x2, local copies, waits for them, and re-layouts, on_device(): a_rows = coef_node.reshape(-1)[local_rows]  45.6 us
    gather x2, local copies, waits for them, and re-layouts, on_device(): load_values = load_field[local_rows]  45.6 us
    psum x1, blocking collectives, on_device(): alpha = rz_now / lax.psum(jnp.sum(direction * image), ('sub', 'coarse'))  39.9 us
    psum x2, blocking collectives, on_device(): column = lax.psum(apply_term, 'sub')  38.2 us
    ppermute x6, starting transfers between devices, padded_2(): after = lax.ppermute(leading, axis, down)  18.7 us
  transfers between devices with their start and end apart: 12, of which 8 were waited for; matrix products, arithmetic and copies ran while one was open for 0% of the time, Pallas kernels for 0%

commit v1 on v0

v1 whole, which is shorter than its diff:
```python
import functools

import jax
import jax.numpy as jnp
from jax import lax
from jax.experimental import pallas as pl
from jax.experimental.pallas import tpu as pltpu
from jax.sharding import PartitionSpec as P

ITERS = 2
CHUNK = 512
BF = jnp.bfloat16
F32 = jnp.float32
HI = lax.Precision.HIGHEST
MESH = pl.DeviceIdType.MESH


def exact_dot(a, b):
    return jnp.dot(a, b, precision=HI, preferred_element_type=F32)


def halves(x):
    high = x.astype(BF)
    return high, (x - high.astype(F32)).astype(BF)


def iota(shape, dim):
    return lax.broadcasted_iota(jnp.int32, shape, dim)


def each(low, high, body):
    if high - low <= 8:
        for i in range(low, high):
            body(i)
    else:
        lax.fori_loop(low, high, lambda i, c: (body(i), c)[1], 0)


def right_operand(x):
    high, low = halves(x)
    return jnp.concatenate([high, low, high], axis=0)


def left_operand(x):
    high, low = halves(x)
    return jnp.concatenate([high, high, low], axis=1)


def times(x, right):
    return jnp.dot(left_operand(x), right, preferred_element_type=F32)


def kernel(
    n_sub,
    n_col,
    loads,
    mode_x,
    mode_y,
    mode_z,
    eigen,
    classes,
    coefficients,
    partner,
    rows,
    corner_id,
    corner_row,
    cinv,
    out_mult,
    out_resid,
    onehot,
    node_z,
    el_ref,
    pair_f,
    pair_b,
    side_f,
    side_b,
    lam_ref,
    root_ref,
    corner_l,
    pad_ref,
    cfull,
    send_v,
    recv_v,
    vec_sub,
    vec_col,
    mine_col,
    send_sem,
    recv_sem,
    sub_send,
    sub_recv,
    col_send,
    col_recv,
    cinv_send,
    cinv_recv,
):
    me = lax.axis_index("sub")
    col = lax.axis_index("coarse")
    size_x = mode_x.shape[2]
    size_y = mode_y.shape[2]
    size_z = mode_z.shape[2]
    plane = size_x * size_y
    width = rows.shape[3]
    corners = corner_row.shape[2]
    total_corners = cinv.shape[1]
    padded = vec_sub.shape[3]
    z_shift = size_z.bit_length() - 1

    barrier = pltpu.get_barrier_semaphore()

    def greet_sub(s):
        pl.semaphore_signal(
            barrier, inc=1, device_id=(lax.rem(me + s, n_sub), col), device_id_type=MESH
        )

    def greet_col(s):
        pl.semaphore_signal(
            barrier, inc=1, device_id=(me, lax.rem(col + s, n_col)), device_id_type=MESH
        )

    each(1, n_sub, greet_sub)
    each(1, n_col, greet_col)

    spots = (
        (lax.rem(me + 1, n_sub), col),
        (lax.rem(me + n_sub - 1, n_sub), col),
        (me, lax.rem(col + 1, n_col)),
        (me, lax.rem(col + n_col - 1, n_col)),
    )
    opposite = (1, 0, 3, 2)
    signs = [
        jnp.where(me * n_col + col < s * n_col + c, 1.0, -1.0).astype(F32) for s, c in spots
    ]
    match = [
        [
            jnp.where(
                jnp.logical_and(partner[0, 0, k, 0] == s, partner[0, 0, k, 1] == c), 1, 0
            ).astype(jnp.int32)
            for k in range(4)
        ]
        for s, c in spots
    ]

    for d in range(4):
        picked = match[d][0] * rows[0, 0, 0:1, :]
        for k in range(1, 4):
            picked = picked + match[d][k] * rows[0, 0, k : k + 1, :]
        node_z[d] = lax.bitwise_and(picked, size_z - 1)
        above = lax.shift_right_logical(picked, z_shift)
        for at in range(0, width, CHUNK):
            hit = iota((plane, CHUNK), 0) == above[:, at : at + CHUNK]
            onehot[d, :, at : at + CHUNK] = jnp.where(hit, 1.0, 0.0).astype(BF)

    size_bz = classes.shape[4]
    blocks_y = classes.shape[3]
    blocks_x = classes.shape[2]
    el_ref[...] = jnp.zeros_like(el_ref)
    for bx in range(blocks_x):
        ids = classes[0, 0, bx]
        value = jnp.zeros(ids.shape, F32)
        for n in range(coefficients.shape[0]):
            value = jnp.where(ids == n, coefficients[n], value)
        el_ref[bx * blocks_y : (bx + 1) * blocks_y, 0:size_bz] = value
    el_t = el_ref[...].T[:size_bz, : blocks_x * blocks_y]
    plane_at = iota((blocks_x * blocks_y, plane), 1)
    block_at = (plane_at // (4 * size_y)) * blocks_y + (plane_at % size_y) // 4
    spread = jnp.where(iota((blocks_x * blocks_y, plane), 0) == block_at, 1.0, 0.0)
    coef_block = exact_dot(el_t, spread)
    spread_z = jnp.where(
        iota((size_z, size_bz), 0) // 4 == iota((size_z, size_bz), 1), 1.0, 0.0
    )
    root = exact_dot(spread_z, 1.0 / jnp.sqrt(coef_block))
    root_ref[...] = root

    def copy_of(turn, d):
        return pltpu.make_async_remote_copy(
            src_ref=send_v.at[turn, d],
            dst_ref=recv_v.at[turn, opposite[d]],
            send_sem=send_sem.at[turn, d],
            recv_sem=recv_sem.at[turn, opposite[d]],
            device_id=spots[d],
            device_id_type=MESH,
        )

    def gather(turn, field, shift):
        depth = field.shape[0]
        high, low = halves(field)
        stacked = jnp.concatenate([high, low], axis=0)
        for d in range(4):
            for at in range(0, width, CHUNK):
                part = jnp.dot(
                    stacked, onehot[d, :, at : at + CHUNK], preferred_element_type=F32
                )
                part = part[:depth] + part[depth:]
                at_z = lax.shift_right_logical(node_z[d, :, at : at + CHUNK], shift)
                hit = iota((depth, CHUNK), 0) == at_z
                send_v[turn, d, :, at : at + CHUNK] = jnp.sum(
                    jnp.where(hit, part, 0.0), axis=0, keepdims=True
                )
            copy_of(turn, d).start()

    pl.semaphore_wait(barrier, n_sub - 1 + n_col - 1)

    def cinv_copy(s):
        return pltpu.make_async_remote_copy(
            src_ref=cinv,
            dst_ref=cfull.at[col],
            send_sem=cinv_send.at[s],
            recv_sem=cinv_recv.at[s],
            device_id=(me, lax.rem(col + s, n_col)),
            device_id_type=MESH,
        )

    each(1, n_col, lambda s: cinv_copy(s).start())
    cfull[col] = cinv[...]
    gather(0, coef_block, 2)

    def expand(mode, by_row, by_col):
        size = mode.shape[0]
        left = jnp.where(by_row(iota((plane, size), 0)) == iota((plane, size), 1), 1.0, 0.0)
        right = jnp.where(by_col(iota((size, plane), 1)) == iota((size, plane), 0), 1.0, 0.0)
        return exact_dot(exact_dot(left, mode), right)

    pair = expand(mode_x[0, 0], lambda i: i // size_y, lambda i: i // size_y) * expand(
        mode_y[0, 0], lambda i: i % size_y, lambda i: i % size_y
    )
    side = mode_z[0, 0]
    pair_f[...] = right_operand(pair)
    pair_b[...] = right_operand(pair.T)
    side_f[...] = left_operand(side.T)
    side_b[...] = left_operand(side)

    spectrum = eigen[0]
    modes = spectrum.shape[1]
    mode_at = iota((modes, plane), 0)
    to_plane = jnp.logical_or(
        mode_at == iota((modes, plane), 1) // size_y,
        mode_at == size_x + iota((modes, plane), 1) % size_y,
    )
    plane_eigen = exact_dot(
        jnp.broadcast_to(spectrum, (8, modes)), jnp.where(to_plane, 1.0, 0.0)
    )[0:1]
    z_at = iota((size_z, modes), 0) + size_x + size_y == iota((size_z, modes), 1)
    z_eigen = jnp.sum(jnp.where(z_at, spectrum, 0.0), axis=1, keepdims=True)
    lam_ref[...] = 1.0 / (z_eigen + plane_eigen)

    def forward(field):
        mixed = times(field * root_ref[...], pair_f[...])
        return jnp.dot(side_f[...], right_operand(mixed), preferred_element_type=F32)

    def backward(spectral):
        mixed = times(spectral, pair_b[...])
        return root_ref[...] * jnp.dot(
            side_b[...], right_operand(mixed), preferred_element_type=F32
        )

    gather(1, backward(lam_ref[...] * forward(loads[0, 0].reshape(plane, size_z).T)), 0)

    lane_z = iota((corners, size_z), 1)
    lane_p = iota((corners, plane), 1)
    lane_n = iota((corners, padded), 1)
    at_z = jnp.zeros((corners, size_z), jnp.int32)
    at_p = jnp.zeros((corners, plane), jnp.int32)
    at_n = jnp.zeros((corners, padded), jnp.int32)
    for t in range(corners):
        node = corner_row[0, 0, t]
        at_z = jnp.where(iota((corners, size_z), 0) == t, node, at_z)
        at_p = jnp.where(iota((corners, plane), 0) == t, node, at_p)
        at_n = jnp.where(iota((corners, padded), 0) == t, corner_id[0, 0, t], at_n)
    pick_z = jnp.where(lax.bitwise_and(at_z, size_z - 1) == lane_z, 1.0, 0.0)
    pick_p = jnp.where(lax.shift_right_logical(at_p, z_shift) == lane_p, 1.0, 0.0)
    pick_n = jnp.where(at_n == lane_n, 1.0, 0.0)
    corner_root = jnp.sum(exact_dot(pick_z, root) * pick_p, axis=1, keepdims=True)
    corner_z = exact_dot(pick_z, side)
    corner_p = exact_dot(pick_p, pair) * corner_root
    high, low = halves(corner_z)
    pad_ref[...] = jnp.zeros_like(pad_ref)
    pad_ref[0:corners, :] = high.astype(F32)
    pad_ref[corners : 2 * corners, :] = high.astype(F32)
    pad_ref[2 * corners : 3 * corners, :] = low.astype(F32)
    corner_l[...] = pad_ref[...].T.astype(BF)
    corner_z3 = jnp.concatenate([high.astype(F32), high.astype(F32), low.astype(F32)], axis=1)
    corner_z3 = corner_z3.astype(BF)

    def all_sum(turn, vector):
        vec_sub[turn, 0] = vector

        def sub_copy(s):
            return pltpu.make_async_remote_copy(
                src_ref=vec_sub.at[turn, 0],
                dst_ref=vec_sub.at[turn, s],
                send_sem=sub_send.at[turn, s],
                recv_sem=sub_recv.at[turn, s],
                device_id=(lax.rem(me + s, n_sub), col),
                device_id_type=MESH,
            )

        def col_copy(s):
            return pltpu.make_async_remote_copy(
                src_ref=mine_col.at[turn],
                dst_ref=vec_col.at[turn, s],
                send_sem=col_send.at[turn, s],
                recv_sem=col_recv.at[turn, s],
                device_id=(me, lax.rem(col + s, n_col)),
                device_id_type=MESH,
            )

        each(1, n_sub, lambda s: sub_copy(s).start())
        each(1, n_sub, lambda s: sub_copy(s).wait())
        mine = jnp.sum(vec_sub[turn], axis=0)
        mine_col[turn] = mine
        each(1, n_col, lambda s: col_copy(s).start())
        vec_col[turn, 0] = mine
        each(1, n_col, lambda s: col_copy(s).wait())
        return jnp.sum(vec_col[turn], axis=0)

    def receive(turn):
        for d in range(4):
            copy_of(turn, d).wait()

    def jump(turn):
        receive(turn)
        return [signs[d] * (send_v[turn, d] - recv_v[turn, d]) for d in range(4)]

    def scatter(values):
        total = jnp.zeros((2 * size_z, plane), F32)
        for d in range(4):
            scaled = signs[d] * values[d]
            high = scaled.astype(BF).astype(F32)
            low = scaled - high
            for at in range(0, width, CHUNK):
                hit = iota((size_z, CHUNK), 0) == node_z[d, :, at : at + CHUNK]
                stacked = jnp.concatenate(
                    [
                        jnp.where(hit, high[:, at : at + CHUNK], 0.0).astype(BF),
                        jnp.where(hit, low[:, at : at + CHUNK], 0.0).astype(BF),
                    ],
                    axis=0,
                )
                total = total + lax.dot_general(
                    stacked,
                    onehot[d, :, at : at + CHUNK],
                    (((1,), (1,)), ((), ())),
                    preferred_element_type=F32,
                )
        return total[:size_z] + total[size_z:]

    def all_of(x):
        return jnp.sum(jnp.sum(x, axis=0, keepdims=True), axis=1, keepdims=True)

    def dot4(a, b):
        total = a[0] * b[0]
        for d in range(1, 4):
            total = total + a[d] * b[d]
        return jnp.sum(total, axis=1, keepdims=True)

    first_row = iota((corners, padded), 0) == 0

    def apply(turn, values, scalars):
        modal = forward(scatter(values))
        spectral = lam_ref[...] * modal
        energy = all_of(modal * spectral)
        at_corner = jnp.sum(
            jnp.dot(corner_z3, right_operand(spectral), preferred_element_type=F32) * corner_p,
            axis=1,
            keepdims=True,
        )
        vector = pick_n * at_corner
        for n, scalar in enumerate([energy] + scalars):
            here = jnp.logical_and(first_row, lane_n == total_corners + n)
            vector = jnp.where(here, scalar, vector)
        summed = all_sum(turn - 2, vector)
        if turn == 2:
            each(1, n_col, lambda s: cinv_copy(s).wait())
        inverse = cfull[...].reshape(total_corners, total_corners)
        coarse = jnp.sum(exact_dot(summed[:, :total_corners], inverse), axis=0, keepdims=True)
        total = jnp.sum(summed, axis=0, keepdims=True)
        quad = jnp.sum(total[:, :total_corners] * coarse, axis=1, keepdims=True)
        local = jnp.sum(pick_n[:, :total_corners] * coarse, axis=1, keepdims=True)
        high, low = halves(corner_p * local)
        high, low = high.astype(F32), low.astype(F32)
        rest = jnp.zeros((size_z - 3 * corners, plane), F32)
        source = jnp.concatenate([high, low, high, rest], axis=0).astype(BF)
        extra = jnp.dot(corner_l[...], source, preferred_element_type=F32)
        gather(turn, backward(spectral + lam_ref[...] * extra), 0)
        lane = iota((1, padded), 1)
        got = [
            jnp.sum(jnp.where(lane == total_corners + n, total, 0.0), axis=1, keepdims=True)
            for n in range(1 + len(scalars))
        ]
        return 2.0 * (got[0] + quad), got[1:]

    receive(0)
    weight = []
    for d in range(4):
        near, far = send_v[0, d], recv_v[0, d]
        weight.append(near * far / (near + far))
    four = range(4)
    resid = jump(1)
    direction = [weight[d] * resid[d] for d in four]
    image_dot, (rz,) = apply(2, direction, [dot4(resid, direction)])
    alpha = rz / image_dot
    mult = [alpha * direction[d] for d in four]
    image = jump(2)
    for step in range(1, ITERS):
        resid = [resid[d] - alpha * image[d] for d in four]
        precond = [weight[d] * resid[d] for d in four]
        own_dot, (rz_next, cross) = apply(
            2 + step, precond, [dot4(resid, precond), dot4(precond, image)]
        )
        beta = rz_next / rz
        image_dot = own_dot + 2.0 * beta * cross + beta * beta * image_dot
        alpha = rz_next / image_dot
        rz = rz_next
        direction = [precond[d] + beta * direction[d] for d in four]
        mult = [mult[d] + alpha * direction[d] for d in four]
        fresh = jump(2 + step)
        image = [fresh[d] + beta * image[d] for d in four]
    resid = [resid[d] - alpha * image[d] for d in four]
    for k in range(4):
        share = [match[d][k].astype(F32) for d in four]
        one = share[0] * mult[0]
        two = share[0] * resid[0]
        for d in range(1, 4):
            one = one + share[d] * mult[d]
            two = two + share[d] * resid[d]
        out_mult[0, 0, k : k + 1, :] = one
        out_resid[0, 0, k : k + 1, :] = two


def on_device(n_sub, n_col, *args):
    loads, mode_x, mode_y, mode_z, eigen, classes = args[:6]
    rows, cinv = args[8], args[11]
    size_z = mode_z.shape[2]
    plane = mode_x.shape[2] * mode_y.shape[2]
    width = rows.shape[3]
    corners = args[10].shape[2]
    total_corners = cinv.shape[1]
    padded = -(-(total_corners + 3) // 128) * 128
    turns = 2 + ITERS
    vmem = pl.BlockSpec(memory_space=pltpu.VMEM)
    smem = pl.BlockSpec(memory_space=pltpu.SMEM)
    dma = pltpu.SemaphoreType.DMA
    out = jax.ShapeDtypeStruct(rows.shape, F32)
    return pl.pallas_call(
        functools.partial(kernel, n_sub, n_col),
        out_shape=(out, out),
        in_specs=[vmem] * 6 + [smem] * 2 + [vmem] + [smem] * 2 + [vmem],
        out_specs=(vmem, vmem),
        scratch_shapes=[
            pltpu.VMEM((4, plane, width), BF),
            pltpu.VMEM((4, 1, width), jnp.int32),
            pltpu.VMEM((128, 128), F32),
            pltpu.VMEM((3 * plane, plane), BF),
            pltpu.VMEM((3 * plane, plane), BF),
            pltpu.VMEM((size_z, 3 * size_z), BF),
            pltpu.VMEM((size_z, 3 * size_z), BF),
            pltpu.VMEM((size_z, plane), F32),
            pltpu.VMEM((size_z, plane), F32),
            pltpu.VMEM((size_z, size_z), BF),
            pltpu.VMEM((size_z, size_z), F32),
            pltpu.VMEM((n_col,) + cinv.shape, F32),
            pltpu.VMEM((turns, 4, 1, width), F32),
            pltpu.VMEM((turns, 4, 1, width), F32),
            pltpu.VMEM((ITERS, n_sub, corners, padded), F32),
            pltpu.VMEM((ITERS, n_col, corners, padded), F32),
            pltpu.VMEM((ITERS, corners, padded), F32),
            dma((turns, 4)),
            dma((turns, 4)),
            dma((ITERS, n_sub)),
            dma((ITERS, n_sub)),
            dma((ITERS, n_col)),
            dma((ITERS, n_col)),
            dma((n_col,)),
            dma((n_col,)),
        ],
        compiler_params=pltpu.CompilerParams(
            collective_id=0, has_side_effects=True, vmem_limit_bytes=48 * 1024 * 1024
        ),
        name="feti_pcg",
    )(*args)


def solution(mesh):
    placed = (
        P("sub", "coarse", None, None, None),
        P("sub", "coarse", None, None),
        P("sub", "coarse", None, None),
        P("sub", "coarse", None, None),
        P("sub", "coarse", None),
        P("sub", "coarse", None, None, None),
        P(),
        P("sub", "coarse", None, None),
        P("sub", "coarse", None, None),
        P("sub", "coarse", None),
        P("sub", "coarse", None),
        P("coarse", None),
    )
    return jax.shard_map(
        functools.partial(on_device, mesh.shape["sub"], mesh.shape["coarse"]),
        mesh=mesh,
        in_specs=placed,
        out_specs=(P("sub", "coarse", None, None), P("sub", "coarse", None, None)),
        check_vma=False,
    )
```

time: 505 us -> 53.9 us (0.11)
  local copies, waits for them, and re-layouts: 261 us -> 7.31 us
  blocking collectives: 184 us -> 0 us
  Pallas kernels: 0 us -> 45.1 us
  starting transfers between devices: 20.9 us -> 0 us
  waiting for transfers between devices: 18.3 us -> 0 us
  matrix products: 7.8 us -> 0 us
  other arithmetic: 5.72 us -> 0 us
  between operations: 5.77 us -> 0.69 us
    gather x12 -> x0, local copies, waits for them, and re-layouts: 185 us -> none  [the longest x4 91.1 us: on_device(): apply_values = (local + solve(extra))[local_rows]]
    psum x7 -> x0, blocking collectives: 171 us -> none  [the longest x2 81.4 us: precond_dot(): return lax.psum(jnp.sum(resid * pre), ('sub', 'coarse'))]
    scatter x4 -> x0, local copies, waits for them, and re-layouts: 62.5 us -> none  [the longest x2 61 us: on_device(): jnp.zeros((nodes,), jnp.float32).at[flat_rows]]
    pallas_call x0 -> x1, Pallas kernels: none -> 45.1 us  [on_device(): pl.pallas_call(functools.partial(kernel, n_sub, n_col), out_shape=(out, o...]
    ppermute x12 -> x0, starting transfers between devices: 20.9 us -> none  [the longest x6 18.7 us: padded_2(): after = lax.ppermute(leading, axis, down)]
    ppermute x12 -> x0, waiting for transfers between devices: 18.3 us -> none  [the longest x6 17 us: padded_2(): before = lax.ppermute(last, axis, up)]
    unnamed x2 -> x0, blocking collectives: 13.1 us -> none
    dot_general x22 -> x0, matrix products: 7.8 us -> none  [the longest x5 2.96 us: solve(): jnp.einsum('pa,pz->az', side_pair, values, precision=lax.Precision.HIGHEST)]
  transfers between devices with their start and end apart: 12 -> 0, of which waited for: 8 -> 0; matrix products, arithmetic and copies ran while one was open for 0% -> 0% of each run, Pallas kernels for 0% -> 0%
where the time goes in v1:
time: 53.9 us; the launch traced here: 53.1 us
  Pallas kernels  45.1 us (84%)
  local copies, waits for them, and re-layouts  7.31 us (14%)
  between operations  0.69 us (1%)
    pallas_call x1, Pallas kernels, on_device(): pl.pallas_call(functools.partial(kernel, n_sub, n_col), out_shape=(out, o...  45.1 us
    unnamed x25, local copies, waits for them, and re-layouts  7.31 us

profile of v1, /device:TPU:0, one launch (start us, length us, event | category | flops | bytes accessed | tf_op | source)
XLA Modules:
  0.0 53.1 jit_solution(2567888577874125754)
XLA Ops:
  0.6 0.0 copy-start.10
  0.6 0.0 copy-start.9
  0.7 0.0 copy-start.8
  0.7 0.0 copy-start.7
  0.7 0.8 %copy.14.partner = s32[1,1,4,2]{3,2,1,0:T(4,128)S(1)} copy(s32[1,1,4,2]{2,3,1,0:T(2,128)} %param.19) | data formatting | bytes 64 | tf_op args[7]
  1.5 0.0 copy-done.10
  1.5 0.0 copy-done.9
  1.5 0.0 copy-done.8
  1.5 0.0 copy-done.7
  1.5 0.0 copy-start
  1.5 0.9 %copy-done = f32[1,1,16,16,128]{4,3,2,1,0:T(8,128)S(1)} copy-done((f32[1,1,16,16,128]{4,3,2,1,0:T(8,128)S(1)}, f32[1,1,16,16,128]{4,3,2,1,0:T(8,128)}, u32[]{:S(2)}) %copy-start) | copy-done | bytes 131096
  2.4 0.0 copy-start.1
  2.4 0.8 %copy-done.1 = f32[1,1,128,128]{3,2,1,0:T(8,128)S(1)} copy-done((f32[1,1,128,128]{3,2,1,0:T(8,128)S(1)}, f32[1,1,128,128]{3,2,1,0:T(8,128)}, u32[]{:S(2)}) %copy-start.1) | copy-done | bytes 65560
  3.2 0.0 copy-start.2
  3.2 0.8 %copy-done.2 = s32[1,1,4,2048]{3,2,1,0:T(4,128)S(1)} copy-done((s32[1,1,4,2048]{3,2,1,0:T(4,128)S(1)}, s32[1,1,4,2048]{3,2,1,0:T(4,128)}, u32[]{:S(2)}) %copy-start.2) | copy-done | bytes 32792
  4.0 0.0 copy-start.3
  4.0 0.7 %copy-done.3 = f32[1,1,16,16]{3,2,1,0:T(8,128)S(1)} copy-done((f32[1,1,16,16]{3,2,1,0:T(8,128)S(1)}, f32[1,1,16,16]{3,2,1,0:T(8,128)}, u32[]{:S(2)}) %copy-start.3) | copy-done | bytes 1048
  4.7 0.0 copy-start.4
  4.7 0.7 %copy-done.4 = f32[1,1,16,16]{3,2,1,0:T(8,128)S(1)} copy-done((f32[1,1,16,16]{3,2,1,0:T(8,128)S(1)}, f32[1,1,16,16]{3,2,1,0:T(8,128)}, u32[]{:S(2)}) %copy-start.4) | copy-done | bytes 1048
  5.4 0.0 copy-start.5
  5.4 0.7 %copy-done.5 = s32[1,1,4,4,32]{4,3,2,1,0:T(4,128)S(1)} copy-done((s32[1,1,4,4,32]{4,3,2,1,0:T(4,128)S(1)}, s32[1,1,4,4,32]{4,3,2,1,0:T(4,128)}, u32[]{:S(2)}) %copy-start.5) | copy-done | bytes 2072
  6.1 0.0 copy-start.6
  6.1 0.7 %copy-done.6 = f32[8,32]{1,0:T(8,128)S(1)} copy-done((f32[8,32]{1,0:T(8,128)S(1)}, f32[8,32]{1,0:T(8,128)}, u32[]{:S(2)}) %copy-start.6) | copy-done | bytes 1048
  6.8 45.1 %feti_pcg.1 = (f32[1,1,4,2048]{3,2,1,0:T(4,128)S(1)}, f32[1,1,4,2048]{3,2,1,0:T(4,128)S(1)}) custom-call(f32[1,1,16,16,128]{4,3,2,1,0:T(8,128)S(1)} %copy-done, f32[1,1,16,16]{3,2,1,0:T(8,128)S(1)} %copy-done.3, f32[1,1,16,16]{3,2,1,0:T(8,128)S(1)} %copy-done.4, f32[1,1,128,128]{3,2,1,0:T(8,128)S(1)} %copy-done.1, f32[1,1,160]{2,1,0:T(1,128)S(1)} %copy-done.7, ...), custom_call_target="tpu_custom_call" | custom-call | tf_op jit(solution)/shard_map/feti_pcg/pallas_call | solution.py:444
  51.9 0.6 %copy.17 = f32[1,1,4,2048]{3,2,1,0:T(4,128)} copy(f32[1,1,4,2048]{3,2,1,0:T(4,128)S(1)} %get-tuple-element.4) | data formatting | bytes 65536
  52.5 0.6 %copy.18 = f32[1,1,4,2048]{3,2,1,0:T(4,128)} copy(f32[1,1,4,2048]{3,2,1,0:T(4,128)S(1)} %get-tuple-element.5) | data formatting | bytes 65536
Async XLA Ops:
  0.6 0.8 %copy-start.10 = (s32[1,1,8]{2,1,0:T(1,128)S(1)}, s32[1,1,8]{2,1,0:T(1,128)}, u32[]{:S(2)}) copy-start(s32[1,1,8]{2,1,0:T(1,128)} %corner_row.1) | copy-start | bytes 100
  0.6 0.8 %copy-start.9 = (s32[1,1,8]{2,1,0:T(1,128)S(1)}, s32[1,1,8]{2,1,0:T(1,128)}, u32[]{:S(2)}) copy-start(s32[1,1,8]{2,1,0:T(1,128)} %corner_id.1) | copy-start | bytes 100
  0.7 0.8 %copy-start.8 = (f32[16]{0:T(128)S(1)}, f32[16]{0:T(128)}, u32[]{:S(2)}) copy-start(f32[16]{0:T(128)} %coefficients.1) | copy-start | bytes 196
  0.7 0.8 %copy-start.7 = (f32[1,1,160]{2,1,0:T(1,128)S(1)}, f32[1,1,160]{2,1,0:T(1,128)}, u32[]{:S(2)}) copy-start(f32[1,1,160]{2,1,0:T(1,128)} %eigen.1) | copy-start | bytes 1924
  1.5 0.9 %copy-start = (f32[1,1,16,16,128]{4,3,2,1,0:T(8,128)S(1)}, f32[1,1,16,16,128]{4,3,2,1,0:T(8,128)}, u32[]{:S(2)}) copy-start(f32[1,1,16,16,128]{4,3,2,1,0:T(8,128)} %loads.1) | copy-start | bytes 393220
  2.4 0.8 %copy-start.1 = (f32[1,1,128,128]{3,2,1,0:T(8,128)S(1)}, f32[1,1,128,128]{3,2,1,0:T(8,128)}, u32[]{:S(2)}) copy-start(f32[1,1,128,128]{3,2,1,0:T(8,128)} %mode_z.1) | copy-start | bytes 196612
  3.2 0.8 %copy-start.2 = (s32[1,1,4,2048]{3,2,1,0:T(4,128)S(1)}, s32[1,1,4,2048]{3,2,1,0:T(4,128)}, u32[]{:S(2)}) copy-start(s32[1,1,4,2048]{3,2,1,0:T(4,128)} %rows.1) | copy-start | bytes 98308
  4.0 0.7 %copy-start.3 = (f32[1,1,16,16]{3,2,1,0:T(8,128)S(1)}, f32[1,1,16,16]{3,2,1,0:T(8,128)}, u32[]{:S(2)}) copy-start(f32[1,1,16,16]{3,2,1,0:T(8,128)} %mode_x.1) | copy-start | bytes 3076
  4.7 0.7 %copy-start.4 = (f32[1,1,16,16]{3,2,1,0:T(8,128)S(1)}, f32[1,1,16,16]{3,2,1,0:T(8,128)}, u32[]{:S(2)}) copy-start(f32[1,1,16,16]{3,2,1,0:T(8,128)} %mode_y.1) | copy-start | bytes 3076
  5.4 0.7 %copy-start.5 = (s32[1,1,4,4,32]{4,3,2,1,0:T(4,128)S(1)}, s32[1,1,4,4,32]{4,3,2,1,0:T(4,128)}, u32[]{:S(2)}) copy-start(s32[1,1,4,4,32]{4,3,2,1,0:T(4,128)} %classes.1) | copy-start | bytes 6148
  6.1 0.7 %copy-start.6 = (f32[8,32]{1,0:T(8,128)S(1)}, f32[8,32]{1,0:T(8,128)}, u32[]{:S(2)}) copy-start(f32[8,32]{1,0:T(8,128)} %cinv.1) | copy-start | bytes 3076

commit v2 on v1

--- a/solution.py
+++ b/solution.py
@@ -53,21 +53,32 @@
 def kernel(
     n_sub,
     n_col,
+    loads_hbm,
+    mode_x_hbm,
+    mode_y_hbm,
+    mode_z_hbm,
+    eigen_hbm,
+    classes_hbm,
+    coefficients,
+    partner,
+    rows_hbm,
+    corner_id,
+    corner_row,
+    cinv_hbm,
+    out_mult,
+    out_resid,
     loads,
     mode_x,
     mode_y,
     mode_z,
     eigen,
     classes,
-    coefficients,
-    partner,
     rows,
-    corner_id,
-    corner_row,
     cinv,
-    out_mult,
-    out_resid,
+    load_sem,
     onehot,
+    masks,
+    placed_rows,
     node_z,
     el_ref,
     pair_f,
@@ -104,7 +115,26 @@
     total_corners = cinv.shape[1]
     padded = vec_sub.shape[3]
     z_shift = size_z.bit_length() - 1
-
+    y_shift = size_y.bit_length() - 1
+    assert size_z == 1 << z_shift and size_y == 1 << y_shift
+
+    fetches = [
+        pltpu.make_async_copy(source, target, load_sem.at[n])
+        for n, (source, target) in enumerate(
+            (
+                (rows_hbm, rows),
+                (classes_hbm, classes),
+                (cinv_hbm, cinv),
+                (mode_x_hbm, mode_x),
+                (mode_y_hbm, mode_y),
+                (mode_z_hbm, mode_z),
+                (eigen_hbm, eigen),
+                (loads_hbm, loads),
+            )
+        )
+    ]
+    for fetch in fetches:
+        fetch.start()
     barrier = pltpu.get_barrier_semaphore()
 
     def greet_sub(s):
@@ -133,12 +163,15 @@
     match = [
         [
             jnp.where(
-                jnp.logical_and(partner[0, 0, k, 0] == s, partner[0, 0, k, 1] == c), 1, 0
+                jnp.logical_and(partner[0, 0, 0, k] == s, partner[0, 0, 1, k] == c), 1, 0
             ).astype(jnp.int32)
             for k in range(4)
         ]
         for s, c in spots
     ]
+
+    for fetch in fetches:
+        fetch.wait()
 
     for d in range(4):
         picked = match[d][0] * rows[0, 0, 0:1, :]
@@ -148,7 +181,10 @@
         above = lax.shift_right_logical(picked, z_shift)
         for at in range(0, width, CHUNK):
             hit = iota((plane, CHUNK), 0) == above[:, at : at + CHUNK]
-            onehot[d, :, at : at + CHUNK] = jnp.where(hit, 1.0, 0.0).astype(BF)
+            here = slice(d * width + at, d * width + at + CHUNK)
+            onehot[:, here] = jnp.where(hit, 1.0, 0.0).astype(BF)
+            hit = iota((size_z, CHUNK), 0) == node_z[d, :, at : at + CHUNK]
+            masks[:, here] = jnp.where(hit, 1.0, 0.0).astype(BF)
 
     size_bz = classes.shape[4]
     blocks_y = classes.shape[3]
@@ -162,11 +198,12 @@
         el_ref[bx * blocks_y : (bx + 1) * blocks_y, 0:size_bz] = value
     el_t = el_ref[...].T[:size_bz, : blocks_x * blocks_y]
     plane_at = iota((blocks_x * blocks_y, plane), 1)
-    block_at = (plane_at // (4 * size_y)) * blocks_y + (plane_at % size_y) // 4
+    block_at = lax.shift_right_logical(plane_at, y_shift + 2) * blocks_y
+    block_at = block_at + lax.shift_right_logical(lax.bitwise_and(plane_at, size_y - 1), 2)
     spread = jnp.where(iota((blocks_x * blocks_y, plane), 0) == block_at, 1.0, 0.0)
     coef_block = exact_dot(el_t, spread)
     spread_z = jnp.where(
-        iota((size_z, size_bz), 0) // 4 == iota((size_z, size_bz), 1), 1.0, 0.0
+        lax.shift_right_logical(iota((size_z, size_bz), 0), 2) == iota((size_z, size_bz), 1), 1.0, 0.0
     )
     root = exact_dot(spread_z, 1.0 / jnp.sqrt(coef_block))
     root_ref[...] = root
@@ -188,7 +225,9 @@
         for d in range(4):
             for at in range(0, width, CHUNK):
                 part = jnp.dot(
-                    stacked, onehot[d, :, at : at + CHUNK], preferred_element_type=F32
+                    stacked,
+                    onehot[:, d * width + at : d * width + at + CHUNK],
+                    preferred_element_type=F32,
                 )
                 part = part[:depth] + part[depth:]
                 at_z = lax.shift_right_logical(node_z[d, :, at : at + CHUNK], shift)
@@ -196,6 +235,7 @@
                 send_v[turn, d, :, at : at + CHUNK] = jnp.sum(
                     jnp.where(hit, part, 0.0), axis=0, keepdims=True
                 )
+        for d in range(4):
             copy_of(turn, d).start()
 
     pl.semaphore_wait(barrier, n_sub - 1 + n_col - 1)
@@ -214,15 +254,28 @@
     cfull[col] = cinv[...]
     gather(0, coef_block, 2)
 
-    def expand(mode, by_row, by_col):
+    def of_x(i):
+        return lax.shift_right_logical(i, y_shift)
+
+    def of_y(i):
+        return lax.bitwise_and(i, size_y - 1)
+
+    def expand(mode, of):
         size = mode.shape[0]
-        left = jnp.where(by_row(iota((plane, size), 0)) == iota((plane, size), 1), 1.0, 0.0)
-        right = jnp.where(by_col(iota((size, plane), 1)) == iota((size, plane), 0), 1.0, 0.0)
-        return exact_dot(exact_dot(left, mode), right)
-
-    pair = expand(mode_x[0, 0], lambda i: i // size_y, lambda i: i // size_y) * expand(
-        mode_y[0, 0], lambda i: i % size_y, lambda i: i % size_y
-    )
+        left = jnp.where(of(iota((plane, size), 0)) == iota((plane, size), 1), 1.0, 0.0)
+        right = jnp.where(of(iota((size, plane), 1)) == iota((size, plane), 0), 1.0, 0.0)
+        left, right = left.astype(BF), right.astype(BF)
+        parts = [
+            jnp.dot(
+                jnp.dot(left, part, preferred_element_type=F32).astype(BF),
+                right,
+                preferred_element_type=F32,
+            )
+            for part in halves(mode)
+        ]
+        return parts[0] + parts[1]
+
+    pair = expand(mode_x[0, 0], of_x) * expand(mode_y[0, 0], of_y)
     side = mode_z[0, 0]
     pair_f[...] = right_operand(pair)
     pair_b[...] = right_operand(pair.T)
@@ -233,8 +286,8 @@
     modes = spectrum.shape[1]
     mode_at = iota((modes, plane), 0)
     to_plane = jnp.logical_or(
-        mode_at == iota((modes, plane), 1) // size_y,
-        mode_at == size_x + iota((modes, plane), 1) % size_y,
+        mode_at == of_x(iota((modes, plane), 1)),
+        mode_at == size_x + of_y(iota((modes, plane), 1)),
     )
     plane_eigen = exact_dot(
         jnp.broadcast_to(spectrum, (8, modes)), jnp.where(to_plane, 1.0, 0.0)
@@ -322,26 +375,19 @@
         return [signs[d] * (send_v[turn, d] - recv_v[turn, d]) for d in range(4)]
 
     def scatter(values):
-        total = jnp.zeros((2 * size_z, plane), F32)
         for d in range(4):
-            scaled = signs[d] * values[d]
-            high = scaled.astype(BF).astype(F32)
-            low = scaled - high
+            high, low = halves(signs[d] * values[d])
             for at in range(0, width, CHUNK):
-                hit = iota((size_z, CHUNK), 0) == node_z[d, :, at : at + CHUNK]
-                stacked = jnp.concatenate(
-                    [
-                        jnp.where(hit, high[:, at : at + CHUNK], 0.0).astype(BF),
-                        jnp.where(hit, low[:, at : at + CHUNK], 0.0).astype(BF),
-                    ],
-                    axis=0,
-                )
-                total = total + lax.dot_general(
-                    stacked,
-                    onehot[d, :, at : at + CHUNK],
-                    (((1,), (1,)), ((), ())),
-                    preferred_element_type=F32,
-                )
+                here = slice(d * width + at, d * width + at + CHUNK)
+                mask = masks[:, here]
+                placed_rows[:size_z, here] = mask * high[:, at : at + CHUNK]
+                placed_rows[size_z:, here] = mask * low[:, at : at + CHUNK]
+        total = lax.dot_general(
+            placed_rows[...],
+            onehot[...],
+            (((1,), (1,)), ((), ())),
+            preferred_element_type=F32,
+        )
         return total[:size_z] + total[size_z:]
 
     def all_of(x):
@@ -428,6 +474,8 @@
 
 
 def on_device(n_sub, n_col, *args):
+    args = list(args)
+    args[7] = jnp.swapaxes(args[7], 2, 3)
     loads, mode_x, mode_y, mode_z, eigen, classes = args[:6]
     rows, cinv = args[8], args[11]
     size_z = mode_z.shape[2]
@@ -438,16 +486,24 @@
     padded = -(-(total_corners + 3) // 128) * 128
     turns = 2 + ITERS
     vmem = pl.BlockSpec(memory_space=pltpu.VMEM)
+    hbm = pl.BlockSpec(memory_space=pltpu.HBM)
     smem = pl.BlockSpec(memory_space=pltpu.SMEM)
     dma = pltpu.SemaphoreType.DMA
     out = jax.ShapeDtypeStruct(rows.shape, F32)
     return pl.pallas_call(
         functools.partial(kernel, n_sub, n_col),
         out_shape=(out, out),
-        in_specs=[vmem] * 6 + [smem] * 2 + [vmem] + [smem] * 2 + [vmem],
+        in_specs=[hbm] * 6 + [smem] * 2 + [hbm] + [smem] * 2 + [hbm],
         out_specs=(vmem, vmem),
         scratch_shapes=[
-            pltpu.VMEM((4, plane, width), BF),
+            *[
+                pltpu.VMEM(x.shape, x.dtype)
+                for x in (loads, mode_x, mode_y, mode_z, eigen, classes, rows, cinv)
+            ],
+            dma((8,)),
+            pltpu.VMEM((plane, 4 * width), BF),
+            pltpu.VMEM((size_z, 4 * width), BF),
+            pltpu.VMEM((2 * size_z, 4 * width), BF),
             pltpu.VMEM((4, 1, width), jnp.int32),
             pltpu.VMEM((128, 128), F32),
             pltpu.VMEM((3 * plane, plane), BF),

time: 53.9 us -> 59 us (1.095)
  Pallas kernels: 45.1 us -> 48.7 us
  local copies, waits for them, and re-layouts: 7.31 us -> 9.17 us
    pallas_call x1, Pallas kernels: 45.1 us -> 48.7 us  [on_device(): pl.pallas_call(functools.partial(kernel, n_sub, n_col), out_shape=(out, o...]
    unnamed x25 -> x26, local copies, waits for them, and re-layouts: 7.31 us -> 9.17 us
where the time goes in v2:
time: 59 us; the launch traced here: 58.5 us
  Pallas kernels  48.7 us (83%)
  local copies, waits for them, and re-layouts  9.17 us (16%)
  between operations  0.67 us (1%)
    pallas_call x1, Pallas kernels, on_device(): pl.pallas_call(functools.partial(kernel, n_sub, n_col), out_shape=(out, o...  48.7 us
    unnamed x26, local copies, waits for them, and re-layouts  9.17 us

profile of v2, /device:TPU:0, one launch (start us, length us, event | category | flops | bytes accessed | tf_op | source)
XLA Modules:
  0.0 58.5 jit_solution(12811932192011676334)
XLA Ops:
  0.6 0.0 copy-start.9
  0.6 0.0 copy-start.7
  0.7 0.6 %copy-done.9 = f32[16]{0:T(128)S(1)} copy-done((f32[16]{0:T(128)S(1)}, f32[16]{0:T(128)}, u32[]{:S(2)}) %copy-start.9) | copy-done | bytes 88
  1.3 0.0 copy-done.7
  1.3 0.0 copy-start
  1.3 0.9 %copy-done = f32[1,1,16,16,128]{4,3,2,1,0:T(8,128)S(1)} copy-done((f32[1,1,16,16,128]{4,3,2,1,0:T(8,128)S(1)}, f32[1,1,16,16,128]{4,3,2,1,0:T(8,128)}, u32[]{:S(2)}) %copy-start) | copy-done | bytes 131096
  2.2 0.0 copy-start.1
  2.2 0.8 %copy-done.1 = f32[1,1,128,128]{3,2,1,0:T(8,128)S(1)} copy-done((f32[1,1,128,128]{3,2,1,0:T(8,128)S(1)}, f32[1,1,128,128]{3,2,1,0:T(8,128)}, u32[]{:S(2)}) %copy-start.1) | copy-done | bytes 65560
  3.1 0.0 copy-start.2
  3.1 0.8 %copy-done.2 = s32[1,1,4,2048]{3,2,1,0:T(4,128)S(1)} copy-done((s32[1,1,4,2048]{3,2,1,0:T(4,128)S(1)}, s32[1,1,4,2048]{3,2,1,0:T(4,128)}, u32[]{:S(2)}) %copy-start.2) | copy-done | bytes 32792
  3.8 0.0 copy-start.3
  3.8 0.7 %copy-done.3 = f32[1,1,16,16]{3,2,1,0:T(8,128)S(1)} copy-done((f32[1,1,16,16]{3,2,1,0:T(8,128)S(1)}, f32[1,1,16,16]{3,2,1,0:T(8,128)}, u32[]{:S(2)}) %copy-start.3) | copy-done | bytes 1048
  4.5 0.0 copy-start.4
  4.5 0.7 %copy-done.4 = f32[1,1,16,16]{3,2,1,0:T(8,128)S(1)} copy-done((f32[1,1,16,16]{3,2,1,0:T(8,128)S(1)}, f32[1,1,16,16]{3,2,1,0:T(8,128)}, u32[]{:S(2)}) %copy-start.4) | copy-done | bytes 1048
  5.2 0.0 copy-start.5
  5.2 0.7 %copy-done.5 = s32[1,1,4,4,32]{4,3,2,1,0:T(4,128)S(1)} copy-done((s32[1,1,4,4,32]{4,3,2,1,0:T(4,128)S(1)}, s32[1,1,4,4,32]{4,3,2,1,0:T(4,128)}, u32[]{:S(2)}) %copy-start.5) | copy-done | bytes 2072
  5.9 0.0 copy-start.6
  5.9 0.7 %copy-done.6 = f32[8,32]{1,0:T(8,128)S(1)} copy-done((f32[8,32]{1,0:T(8,128)S(1)}, f32[8,32]{1,0:T(8,128)}, u32[]{:S(2)}) %copy-start.6) | copy-done | bytes 1048
  6.6 0.0 copy-start.8
  6.6 0.7 %copy-done.8 = s32[1,1,4,2]{2,3,1,0:T(2,128)S(1)} copy-done((s32[1,1,4,2]{2,3,1,0:T(2,128)S(1)}, s32[1,1,4,2]{2,3,1,0:T(2,128)}, u32[]{:S(2)}) %copy-start.8) | copy-done | bytes 56
  7.3 0.0 copy-start.10
  7.3 0.7 %copy-done.10 = s32[1,1,8]{2,1,0:T(1,128)S(1)} copy-done((s32[1,1,8]{2,1,0:T(1,128)S(1)}, s32[1,1,8]{2,1,0:T(1,128)}, u32[]{:S(2)}) %copy-start.10) | copy-done | bytes 56
  7.9 0.0 copy-start.11
  8.0 0.7 %copy-done.11 = s32[1,1,8]{2,1,0:T(1,128)S(1)} copy-done((s32[1,1,8]{2,1,0:T(1,128)S(1)}, s32[1,1,8]{2,1,0:T(1,128)}, u32[]{:S(2)}) %copy-start.11) | copy-done | bytes 56
  8.6 48.7 %feti_pcg.1 = (f32[1,1,4,2048]{3,2,1,0:T(4,128)S(1)}, f32[1,1,4,2048]{3,2,1,0:T(4,128)S(1)}) custom-call(f32[1,1,16,16,128]{4,3,2,1,0:T(8,128)S(1)} %copy-done, f32[1,1,16,16]{3,2,1,0:T(8,128)S(1)} %copy-done.3, f32[1,1,16,16]{3,2,1,0:T(8,128)S(1)} %copy-done.4, f32[1,1,128,128]{3,2,1,0:T(8,128)S(1)} %copy-done.1, f32[1,1,160]{2,1,0:T(1,128)S(1)} %copy-done.7, ...), custom_call_target="tpu_custom_call" | custom-call | tf_op jit(solution)/shard_map/feti_pcg/pallas_call | solution.py:493
  57.3 0.6 %copy.16 = f32[1,1,4,2048]{3,2,1,0:T(4,128)} copy(f32[1,1,4,2048]{3,2,1,0:T(4,128)S(1)} %get-tuple-element.4) | data formatting | bytes 65536
  57.9 0.6 %copy.17 = f32[1,1,4,2048]{3,2,1,0:T(4,128)} copy(f32[1,1,4,2048]{3,2,1,0:T(4,128)S(1)} %get-tuple-element.5) | data formatting | bytes 65536
Async XLA Ops:
  0.6 0.7 %copy-start.9 = (f32[16]{0:T(128)S(1)}, f32[16]{0:T(128)}, u32[]{:S(2)}) copy-start(f32[16]{0:T(128)} %coefficients.1) | copy-start | bytes 196
  0.6 0.7 %copy-start.7 = (f32[1,1,160]{2,1,0:T(1,128)S(1)}, f32[1,1,160]{2,1,0:T(1,128)}, u32[]{:S(2)}) copy-start(f32[1,1,160]{2,1,0:T(1,128)} %eigen_hbm.1) | copy-start | bytes 1924
  1.3 0.9 %copy-start = (f32[1,1,16,16,128]{4,3,2,1,0:T(8,128)S(1)}, f32[1,1,16,16,128]{4,3,2,1,0:T(8,128)}, u32[]{:S(2)}) copy-start(f32[1,1,16,16,128]{4,3,2,1,0:T(8,128)} %loads_hbm.1) | copy-start | bytes 393220
  2.2 0.8 %copy-start.1 = (f32[1,1,128,128]{3,2,1,0:T(8,128)S(1)}, f32[1,1,128,128]{3,2,1,0:T(8,128)}, u32[]{:S(2)}) copy-start(f32[1,1,128,128]{3,2,1,0:T(8,128)} %mode_z_hbm.1) | copy-start | bytes 196612
  3.1 0.8 %copy-start.2 = (s32[1,1,4,2048]{3,2,1,0:T(4,128)S(1)}, s32[1,1,4,2048]{3,2,1,0:T(4,128)}, u32[]{:S(2)}) copy-start(s32[1,1,4,2048]{3,2,1,0:T(4,128)} %rows_hbm.1) | copy-start | bytes 98308
  3.8 0.7 %copy-start.3 = (f32[1,1,16,16]{3,2,1,0:T(8,128)S(1)}, f32[1,1,16,16]{3,2,1,0:T(8,128)}, u32[]{:S(2)}) copy-start(f32[1,1,16,16]{3,2,1,0:T(8,128)} %mode_x_hbm.1) | copy-start | bytes 3076
  4.5 0.7 %copy-start.4 = (f32[1,1,16,16]{3,2,1,0:T(8,128)S(1)}, f32[1,1,16,16]{3,2,1,0:T(8,128)}, u32[]{:S(2)}) copy-start(f32[1,1,16,16]{3,2,1,0:T(8,128)} %mode_y_hbm.1) | copy-start | bytes 3076
  5.2 0.7 %copy-start.5 = (s32[1,1,4,4,32]{4,3,2,1,0:T(4,128)S(1)}, s32[1,1,4,4,32]{4,3,2,1,0:T(4,128)}, u32[]{:S(2)}) copy-start(s32[1,1,4,4,32]{4,3,2,1,0:T(4,128)} %classes_hbm.1) | copy-start | bytes 6148
  5.9 0.7 %copy-start.6 = (f32[8,32]{1,0:T(8,128)S(1)}, f32[8,32]{1,0:T(8,128)}, u32[]{:S(2)}) copy-start(f32[8,32]{1,0:T(8,128)} %cinv_hbm.1) | copy-start | bytes 3076
  6.6 0.7 %copy-start.8 = (s32[1,1,4,2]{2,3,1,0:T(2,128)S(1)}, s32[1,1,4,2]{2,3,1,0:T(2,128)}, u32[]{:S(2)}) copy-start(s32[1,1,4,2]{2,3,1,0:T(2,128)} %param.19) | copy-start | bytes 100
  7.3 0.7 %copy-start.10 = (s32[1,1,8]{2,1,0:T(1,128)S(1)}, s32[1,1,8]{2,1,0:T(1,128)}, u32[]{:S(2)}) copy-start(s32[1,1,8]{2,1,0:T(1,128)} %corner_id.1) | copy-start | bytes 100
  7.9 0.7 %copy-start.11 = (s32[1,1,8]{2,1,0:T(1,128)S(1)}, s32[1,1,8]{2,1,0:T(1,128)}, u32[]{:S(2)}) copy-start(s32[1,1,8]{2,1,0:T(1,128)} %corner_row.1) | copy-start | bytes 100

commit v3 on v2

--- a/solution.py
+++ b/solution.py
@@ -170,8 +170,7 @@
         for s, c in spots
     ]
 
-    for fetch in fetches:
-        fetch.wait()
+    fetches[0].wait()
 
     for d in range(4):
         picked = match[d][0] * rows[0, 0, 0:1, :]
@@ -183,12 +182,12 @@
             hit = iota((plane, CHUNK), 0) == above[:, at : at + CHUNK]
             here = slice(d * width + at, d * width + at + CHUNK)
             onehot[:, here] = jnp.where(hit, 1.0, 0.0).astype(BF)
-            hit = iota((size_z, CHUNK), 0) == node_z[d, :, at : at + CHUNK]
-            masks[:, here] = jnp.where(hit, 1.0, 0.0).astype(BF)
 
     size_bz = classes.shape[4]
     blocks_y = classes.shape[3]
     blocks_x = classes.shape[2]
+    for fetch in fetches[1:]:
+        fetch.wait()
     el_ref[...] = jnp.zeros_like(el_ref)
     for bx in range(blocks_x):
         ids = classes[0, 0, bx]
@@ -218,10 +217,9 @@
             device_id_type=MESH,
         )
 
-    def gather(turn, field, shift):
-        depth = field.shape[0]
-        high, low = halves(field)
-        stacked = jnp.concatenate([high, low], axis=0)
+    def gather(fields):
+        stacked = [half for _, field, _ in fields for half in halves(field)]
+        stacked = jnp.concatenate(stacked, axis=0)
         for d in range(4):
             for at in range(0, width, CHUNK):
                 part = jnp.dot(
@@ -229,30 +227,19 @@
                     onehot[:, d * width + at : d * width + at + CHUNK],
                     preferred_element_type=F32,
                 )
-                part = part[:depth] + part[depth:]
-                at_z = lax.shift_right_logical(node_z[d, :, at : at + CHUNK], shift)
-                hit = iota((depth, CHUNK), 0) == at_z
-                send_v[turn, d, :, at : at + CHUNK] = jnp.sum(
-                    jnp.where(hit, part, 0.0), axis=0, keepdims=True
-                )
-        for d in range(4):
-            copy_of(turn, d).start()
-
-    pl.semaphore_wait(barrier, n_sub - 1 + n_col - 1)
-
-    def cinv_copy(s):
-        return pltpu.make_async_remote_copy(
-            src_ref=cinv,
-            dst_ref=cfull.at[col],
-            send_sem=cinv_send.at[s],
-            recv_sem=cinv_recv.at[s],
-            device_id=(me, lax.rem(col + s, n_col)),
-            device_id_type=MESH,
-        )
-
-    each(1, n_col, lambda s: cinv_copy(s).start())
-    cfull[col] = cinv[...]
-    gather(0, coef_block, 2)
+                first = 0
+                for turn, field, shift in fields:
+                    depth = field.shape[0]
+                    both = part[first : first + depth]
+                    both = both + part[first + depth : first + 2 * depth]
+                    first += 2 * depth
+                    at_z = lax.shift_right_logical(node_z[d, :, at : at + CHUNK], shift)
+                    hit = iota((depth, CHUNK), 0) == at_z
+                    send_v[turn, d, :, at : at + CHUNK] = jnp.sum(
+                        jnp.where(hit, both, 0.0), axis=0, keepdims=True
+                    )
+            for turn, _, _ in fields:
+                copy_of(turn, d).start()
 
     def of_x(i):
         return lax.shift_right_logical(i, y_shift)
@@ -306,7 +293,27 @@
             side_b[...], right_operand(mixed), preferred_element_type=F32
         )
 
-    gather(1, backward(lam_ref[...] * forward(loads[0, 0].reshape(plane, size_z).T)), 0)
+    load_field = backward(lam_ref[...] * forward(loads[0, 0].reshape(plane, size_z).T))
+    pl.semaphore_wait(barrier, n_sub - 1 + n_col - 1)
+
+    def cinv_copy(s):
+        return pltpu.make_async_remote_copy(
+            src_ref=cinv,
+            dst_ref=cfull.at[col],
+            send_sem=cinv_send.at[s],
+            recv_sem=cinv_recv.at[s],
+            device_id=(me, lax.rem(col + s, n_col)),
+            device_id_type=MESH,
+        )
+
+    each(1, n_col, lambda s: cinv_copy(s).start())
+    cfull[col] = cinv[...]
+    gather([(0, coef_block, 2), (1, load_field, 0)])
+    for d in range(4):
+        for at in range(0, width, CHUNK):
+            hit = iota((size_z, CHUNK), 0) == node_z[d, :, at : at + CHUNK]
+            here = slice(d * width + at, d * width + at + CHUNK)
+            masks[:, here] = jnp.where(hit, 1.0, 0.0).astype(BF)
 
     lane_z = iota((corners, size_z), 1)
     lane_p = iota((corners, plane), 1)
@@ -427,7 +434,7 @@
         rest = jnp.zeros((size_z - 3 * corners, plane), F32)
         source = jnp.concatenate([high, low, high, rest], axis=0).astype(BF)
         extra = jnp.dot(corner_l[...], source, preferred_element_type=F32)
-        gather(turn, backward(spectral + lam_ref[...] * extra), 0)
+        gather([(turn, backward(spectral + lam_ref[...] * extra), 0)])
         lane = iota((1, padded), 1)
         got = [
             jnp.sum(jnp.where(lane == total_corners + n, total, 0.0), axis=1, keepdims=True)
@@ -530,7 +537,7 @@
             dma((n_col,)),
         ],
         compiler_params=pltpu.CompilerParams(
-            collective_id=0, has_side_effects=True, vmem_limit_bytes=48 * 1024 * 1024
+            collective_id=0, has_side_effects=True, vmem_limit_bytes=60 * 1024 * 1024
         ),
         name="feti_pcg",
     )(*args)

time: 59 us -> 47.4 us (0.80)
  local copies, waits for them, and re-layouts: 9.17 us -> 2 us
  Pallas kernels: 48.7 us -> 44.5 us
    unnamed x26 -> x4, local copies, waits for them, and re-layouts: 9.17 us -> 2 us
    pallas_call x1, Pallas kernels: 48.7 us -> 44.5 us  [on_device(): pl.pallas_call(functools.partial(kernel, n_sub, n_col), out_shape=(out, o...]
where the time goes in v3:
time: 47.4 us; the launch traced here: 47.2 us
  Pallas kernels  44.5 us (94%)
  local copies, waits for them, and re-layouts  2 us (4%)
  between operations  0.65 us (1%)
    pallas_call x1, Pallas kernels, on_device(): pl.pallas_call(functools.partial(kernel, n_sub, n_col), out_shape=(out, o...  44.5 us
    unnamed x4, local copies, waits for them, and re-layouts  2 us

profile of v3, /device:TPU:0, one launch (start us, length us, event | category | flops | bytes accessed | tf_op | source)
XLA Modules:
  0.0 47.2 jit_solution(17718422005409608972)
XLA Ops:
  0.6 44.5 %feti_pcg.1 = (f32[1,1,4,2048]{3,2,1,0:T(4,128)}, f32[1,1,4,2048]{3,2,1,0:T(4,128)}) custom-call(f32[1,1,16,16,128]{4,3,2,1,0:T(8,128)} %loads_hbm.1, f32[1,1,16,16]{3,2,1,0:T(8,128)} %mode_x_hbm.1, f32[1,1,16,16]{3,2,1,0:T(8,128)} %mode_y_hbm.1, f32[1,1,128,128]{3,2,1,0:T(8,128)} %mode_z_hbm.1, f32[1,1,160]{2,1,0:T(1,128)} %eigen_hbm.1, ...), custom_call_target="tpu_custom_call" | custom-call | tf_op jit(solution)/shard_map/feti_pcg/pallas_call | solution.py:500
  45.2 0.0 copy-start
  45.2 1.4 %copy.16 = f32[1,1,4,2048]{3,2,1,0:T(4,128)} copy(f32[1,1,4,2048]{3,2,1,0:T(4,128)} %get-tuple-element.4) | data formatting | bytes 65536
  46.6 0.0 copy-done
  46.6 0.6 %copy.17 = f32[1,1,4,2048]{3,2,1,0:T(4,128)} copy(f32[1,1,4,2048]{3,2,1,0:T(4,128)S(1)} %copy-done) | data formatting | bytes 65536
Async XLA Ops:
  45.2 1.4 %copy-start = (f32[1,1,4,2048]{3,2,1,0:T(4,128)S(1)}, f32[1,1,4,2048]{3,2,1,0:T(4,128)}, u32[]{:S(2)}) copy-start(f32[1,1,4,2048]{3,2,1,0:T(4,128)} %get-tuple-element.5) | copy-start | bytes 98308

commit v4 on v3

--- a/solution.py
+++ b/solution.py
@@ -80,6 +80,8 @@
     masks,
     placed_rows,
     node_z,
+    node_p,
+    scaled,
     el_ref,
     pair_f,
     pair_b,
@@ -156,7 +158,6 @@
         (me, lax.rem(col + 1, n_col)),
         (me, lax.rem(col + n_col - 1, n_col)),
     )
-    opposite = (1, 0, 3, 2)
     signs = [
         jnp.where(me * n_col + col < s * n_col + c, 1.0, -1.0).astype(F32) for s, c in spots
     ]
@@ -177,11 +178,25 @@
         for k in range(1, 4):
             picked = picked + match[d][k] * rows[0, 0, k : k + 1, :]
         node_z[d] = lax.bitwise_and(picked, size_z - 1)
-        above = lax.shift_right_logical(picked, z_shift)
+        node_p[d] = lax.shift_right_logical(picked, z_shift)
+
+    def lanes(d, at):
+        return pl.ds(pl.multiple_of(d * width + at, 128), CHUNK)
+
+    def over_directions(body):
+        lax.fori_loop(0, 4, lambda d, c: (body(d), c)[1], 0)
+
+    def fill_onehot(d):
         for at in range(0, width, CHUNK):
-            hit = iota((plane, CHUNK), 0) == above[:, at : at + CHUNK]
-            here = slice(d * width + at, d * width + at + CHUNK)
-            onehot[:, here] = jnp.where(hit, 1.0, 0.0).astype(BF)
+            hit = iota((plane, CHUNK), 0) == node_p[d, :, at : at + CHUNK]
+            onehot[:, lanes(d, at)] = jnp.where(hit, 1.0, 0.0).astype(BF)
+
+    def fill_masks(d):
+        for at in range(0, width, CHUNK):
+            hit = iota((size_z, CHUNK), 0) == node_z[d, :, at : at + CHUNK]
+            masks[:, lanes(d, at)] = jnp.where(hit, 1.0, 0.0).astype(BF)
+
+    over_directions(fill_onehot)
 
     size_bz = classes.shape[4]
     blocks_y = classes.shape[3]
@@ -208,23 +223,28 @@
     root_ref[...] = root
 
     def copy_of(turn, d):
+        down, along = d % 2, d // 2
+        opposite = d + 1 - 2 * down
+        to_sub = lax.rem(me + (1 - along) * (1 + down * (n_sub - 2)), n_sub)
+        to_col = lax.rem(col + along * (1 + down * (n_col - 2)), n_col)
         return pltpu.make_async_remote_copy(
             src_ref=send_v.at[turn, d],
-            dst_ref=recv_v.at[turn, opposite[d]],
+            dst_ref=recv_v.at[turn, opposite],
             send_sem=send_sem.at[turn, d],
-            recv_sem=recv_sem.at[turn, opposite[d]],
-            device_id=spots[d],
+            recv_sem=recv_sem.at[turn, opposite],
+            device_id=(to_sub, to_col),
             device_id_type=MESH,
         )
 
     def gather(fields):
         stacked = [half for _, field, _ in fields for half in halves(field)]
         stacked = jnp.concatenate(stacked, axis=0)
-        for d in range(4):
+
+        def one(d):
             for at in range(0, width, CHUNK):
                 part = jnp.dot(
                     stacked,
-                    onehot[:, d * width + at : d * width + at + CHUNK],
+                    onehot[:, lanes(d, at)],
                     preferred_element_type=F32,
                 )
                 first = 0
@@ -241,6 +261,8 @@
             for turn, _, _ in fields:
                 copy_of(turn, d).start()
 
+        over_directions(one)
+
     def of_x(i):
         return lax.shift_right_logical(i, y_shift)
 
@@ -309,11 +331,7 @@
     each(1, n_col, lambda s: cinv_copy(s).start())
     cfull[col] = cinv[...]
     gather([(0, coef_block, 2), (1, load_field, 0)])
-    for d in range(4):
-        for at in range(0, width, CHUNK):
-            hit = iota((size_z, CHUNK), 0) == node_z[d, :, at : at + CHUNK]
-            here = slice(d * width + at, d * width + at + CHUNK)
-            masks[:, here] = jnp.where(hit, 1.0, 0.0).astype(BF)
+    over_directions(fill_masks)
 
     lane_z = iota((corners, size_z), 1)
     lane_p = iota((corners, plane), 1)
@@ -383,18 +401,22 @@
 
     def scatter(values):
         for d in range(4):
-            high, low = halves(signs[d] * values[d])
+            scaled[d] = signs[d] * values[d]
+
+        def one(d, total):
+            high, low = halves(scaled[d])
             for at in range(0, width, CHUNK):
-                here = slice(d * width + at, d * width + at + CHUNK)
-                mask = masks[:, here]
-                placed_rows[:size_z, here] = mask * high[:, at : at + CHUNK]
-                placed_rows[size_z:, here] = mask * low[:, at : at + CHUNK]
-        total = lax.dot_general(
-            placed_rows[...],
-            onehot[...],
-            (((1,), (1,)), ((), ())),
-            preferred_element_type=F32,
-        )
+                mask = masks[:, lanes(d, at)]
+                placed_rows[:size_z, at : at + CHUNK] = mask * high[:, at : at + CHUNK]
+                placed_rows[size_z:, at : at + CHUNK] = mask * low[:, at : at + CHUNK]
+            return total + lax.dot_general(
+                placed_rows[...],
+                onehot[:, pl.ds(pl.multiple_of(d * width, 128), width)],
+                (((1,), (1,)), ((), ())),
+                preferred_element_type=F32,
+            )
+
+        total = lax.fori_loop(0, 4, one, jnp.zeros((2 * size_z, plane), F32))
         return total[:size_z] + total[size_z:]
 
     def all_of(x):
@@ -510,8 +532,10 @@
             dma((8,)),
             pltpu.VMEM((plane, 4 * width), BF),
             pltpu.VMEM((size_z, 4 * width), BF),
-            pltpu.VMEM((2 * size_z, 4 * width), BF),
+            pltpu.VMEM((2 * size_z, width), BF),
             pltpu.VMEM((4, 1, width), jnp.int32),
+            pltpu.VMEM((4, 1, width), jnp.int32),
+            pltpu.VMEM((4, 1, width), F32),
             pltpu.VMEM((128, 128), F32),
             pltpu.VMEM((3 * plane, plane), BF),
             pltpu.VMEM((3 * plane, plane), BF),

time: 47.4 us -> 46.8 us (0.987)
  Pallas kernels: 44.5 us -> 43.9 us
    pallas_call x1, Pallas kernels: 44.5 us -> 43.9 us  [on_device(): pl.pallas_call(functools.partial(kernel, n_sub, n_col), out_shape=(out, o...]
where the time goes in v4:
time: 46.8 us; the launch traced here: 46.6 us
  Pallas kernels  43.9 us (94%)
  local copies, waits for them, and re-layouts  2 us (4%)
  between operations  0.65 us (1%)
    pallas_call x1, Pallas kernels, on_device(): pl.pallas_call(functools.partial(kernel, n_sub, n_col), out_shape=(out, o...  43.9 us
    unnamed x4, local copies, waits for them, and re-layouts  2 us

profile of v4, /device:TPU:0, one launch (start us, length us, event | category | flops | bytes accessed | tf_op | source)
XLA Modules:
  0.0 46.6 jit_solution(15303709112001894386)
XLA Ops:
  0.6 43.9 %feti_pcg.1 = (f32[1,1,4,2048]{3,2,1,0:T(4,128)}, f32[1,1,4,2048]{3,2,1,0:T(4,128)}) custom-call(f32[1,1,16,16,128]{4,3,2,1,0:T(8,128)} %loads_hbm.1, f32[1,1,16,16]{3,2,1,0:T(8,128)} %mode_x_hbm.1, f32[1,1,16,16]{3,2,1,0:T(8,128)} %mode_y_hbm.1, f32[1,1,128,128]{3,2,1,0:T(8,128)} %mode_z_hbm.1, f32[1,1,160]{2,1,0:T(1,128)} %eigen_hbm.1, ...), custom_call_target="tpu_custom_call" | custom-call | tf_op jit(solution)/shard_map/feti_pcg/pallas_call | solution.py:522
  44.5 0.0 copy-start
  44.6 1.4 %copy.16 = f32[1,1,4,2048]{3,2,1,0:T(4,128)} copy(f32[1,1,4,2048]{3,2,1,0:T(4,128)} %get-tuple-element.4) | data formatting | bytes 65536
  45.9 0.0 copy-done
  45.9 0.6 %copy.17 = f32[1,1,4,2048]{3,2,1,0:T(4,128)} copy(f32[1,1,4,2048]{3,2,1,0:T(4,128)S(1)} %copy-done) | data formatting | bytes 65536
Async XLA Ops:
  44.5 1.4 %copy-start = (f32[1,1,4,2048]{3,2,1,0:T(4,128)S(1)}, f32[1,1,4,2048]{3,2,1,0:T(4,128)}, u32[]{:S(2)}) copy-start(f32[1,1,4,2048]{3,2,1,0:T(4,128)} %get-tuple-element.5) | copy-start | bytes 98308

commit v5 on v4

--- a/solution.py
+++ b/solution.py
@@ -9,6 +9,7 @@
 
 ITERS = 2
 CHUNK = 512
+DIRECT = 64
 BF = jnp.bfloat16
 F32 = jnp.float32
 HI = lax.Precision.HIGHEST
@@ -92,6 +93,7 @@
     corner_l,
     pad_ref,
     cfull,
+    own_rows,
     send_v,
     recv_v,
     vec_sub,
@@ -149,8 +151,22 @@
             barrier, inc=1, device_id=(me, lax.rem(col + s, n_col)), device_id_type=MESH
         )
 
-    each(1, n_sub, greet_sub)
-    each(1, n_col, greet_col)
+    n_all = n_sub * n_col
+    direct = n_all <= DIRECT
+    own = me * n_col + col
+
+    def other(s):
+        flat = lax.rem(own + s, n_all)
+        return flat // n_col, lax.rem(flat, n_col)
+
+    def greet_all(s):
+        pl.semaphore_signal(barrier, inc=1, device_id=other(s), device_id_type=MESH)
+
+    if direct:
+        each(1, n_all, greet_all)
+    else:
+        each(1, n_sub, greet_sub)
+        each(1, n_col, greet_col)
 
     spots = (
         (lax.rem(me + 1, n_sub), col),
@@ -316,7 +332,7 @@
         )
 
     load_field = backward(lam_ref[...] * forward(loads[0, 0].reshape(plane, size_z).T))
-    pl.semaphore_wait(barrier, n_sub - 1 + n_col - 1)
+    pl.semaphore_wait(barrier, n_all - 1 if direct else n_sub - 1 + n_col - 1)
 
     def cinv_copy(s):
         return pltpu.make_async_remote_copy(
@@ -359,18 +375,33 @@
     corner_z3 = jnp.concatenate([high.astype(F32), high.astype(F32), low.astype(F32)], axis=1)
     corner_z3 = corner_z3.astype(BF)
 
-    def all_sum(turn, vector):
-        vec_sub[turn, 0] = vector
-
-        def sub_copy(s):
+    def sum_copies(turn):
+        count = n_all if direct else n_sub
+
+        def copy(s):
             return pltpu.make_async_remote_copy(
                 src_ref=vec_sub.at[turn, 0],
                 dst_ref=vec_sub.at[turn, s],
                 send_sem=sub_send.at[turn, s],
                 recv_sem=sub_recv.at[turn, s],
-                device_id=(lax.rem(me + s, n_sub), col),
+                device_id=other(s) if direct else (lax.rem(me + s, n_sub), col),
                 device_id_type=MESH,
             )
+
+        return count, copy
+
+    def sum_start(turn, vector):
+        vec_sub[turn, 0] = vector
+        count, copy = sum_copies(turn)
+        each(1, count, lambda s: copy(s).start())
+
+    def sum_finish(turn):
+        count, copy = sum_copies(turn)
+        each(1, count, lambda s: copy(s).wait())
+        mine = jnp.sum(vec_sub[turn], axis=0)
+        if direct:
+            return mine
+        mine_col[turn] = mine
 
         def col_copy(s):
             return pltpu.make_async_remote_copy(
@@ -382,10 +413,6 @@
                 device_id_type=MESH,
             )
 
-        each(1, n_sub, lambda s: sub_copy(s).start())
-        each(1, n_sub, lambda s: sub_copy(s).wait())
-        mine = jnp.sum(vec_sub[turn], axis=0)
-        mine_col[turn] = mine
         each(1, n_col, lambda s: col_copy(s).start())
         vec_col[turn, 0] = mine
         each(1, n_col, lambda s: col_copy(s).wait())
@@ -428,7 +455,7 @@
             total = total + a[d] * b[d]
         return jnp.sum(total, axis=1, keepdims=True)
 
-    first_row = iota((corners, padded), 0) == 0
+    lane = iota((1, padded), 1)
 
     def apply(turn, values, scalars):
         modal = forward(scatter(values))
@@ -439,25 +466,26 @@
             axis=1,
             keepdims=True,
         )
-        vector = pick_n * at_corner
+        vector = jnp.sum(pick_n * at_corner, axis=0, keepdims=True)
         for n, scalar in enumerate([energy] + scalars):
-            here = jnp.logical_and(first_row, lane_n == total_corners + n)
-            vector = jnp.where(here, scalar, vector)
-        summed = all_sum(turn - 2, vector)
+            vector = jnp.where(lane == total_corners + n, scalar, vector)
+        sum_start(turn - 2, vector)
         if turn == 2:
             each(1, n_col, lambda s: cinv_copy(s).wait())
-        inverse = cfull[...].reshape(total_corners, total_corners)
-        coarse = jnp.sum(exact_dot(summed[:, :total_corners], inverse), axis=0, keepdims=True)
-        total = jnp.sum(summed, axis=0, keepdims=True)
-        quad = jnp.sum(total[:, :total_corners] * coarse, axis=1, keepdims=True)
-        local = jnp.sum(pick_n[:, :total_corners] * coarse, axis=1, keepdims=True)
+            inverse = cfull[...].reshape(total_corners, total_corners)
+            own_rows[...] = exact_dot(pick_n[:, :total_corners], inverse)
+        total = sum_finish(turn - 2)
+        at_corners = total[:, :total_corners]
+        local = jnp.sum(own_rows[...] * at_corners, axis=1, keepdims=True)
         high, low = halves(corner_p * local)
         high, low = high.astype(F32), low.astype(F32)
         rest = jnp.zeros((size_z - 3 * corners, plane), F32)
         source = jnp.concatenate([high, low, high, rest], axis=0).astype(BF)
         extra = jnp.dot(corner_l[...], source, preferred_element_type=F32)
         gather([(turn, backward(spectral + lam_ref[...] * extra), 0)])
-        lane = iota((1, padded), 1)
+        inverse = cfull[...].reshape(total_corners, total_corners)
+        coarse = exact_dot(jnp.broadcast_to(at_corners, (8, total_corners)), inverse)[0:1]
+        quad = jnp.sum(at_corners * coarse, axis=1, keepdims=True)
         got = [
             jnp.sum(jnp.where(lane == total_corners + n, total, 0.0), axis=1, keepdims=True)
             for n in range(1 + len(scalars))
@@ -514,6 +542,7 @@
     total_corners = cinv.shape[1]
     padded = -(-(total_corners + 3) // 128) * 128
     turns = 2 + ITERS
+    first = n_sub * n_col if n_sub * n_col <= DIRECT else n_sub
     vmem = pl.BlockSpec(memory_space=pltpu.VMEM)
     hbm = pl.BlockSpec(memory_space=pltpu.HBM)
     smem = pl.BlockSpec(memory_space=pltpu.SMEM)
@@ -546,15 +575,16 @@
             pltpu.VMEM((size_z, size_z), BF),
             pltpu.VMEM((size_z, size_z), F32),
             pltpu.VMEM((n_col,) + cinv.shape, F32),
+            pltpu.VMEM((corners, total_corners), F32),
             pltpu.VMEM((turns, 4, 1, width), F32),
             pltpu.VMEM((turns, 4, 1, width), F32),
-            pltpu.VMEM((ITERS, n_sub, corners, padded), F32),
-            pltpu.VMEM((ITERS, n_col, corners, padded), F32),
-            pltpu.VMEM((ITERS, corners, padded), F32),
+            pltpu.VMEM((ITERS, first, 1, padded), F32),
+            pltpu.VMEM((ITERS, n_col, 1, padded), F32),
+            pltpu.VMEM((ITERS, 1, padded), F32),
             dma((turns, 4)),
             dma((turns, 4)),
-            dma((ITERS, n_sub)),
-            dma((ITERS, n_sub)),
+            dma((ITERS, first)),
+            dma((ITERS, first)),
             dma((ITERS, n_col)),
             dma((ITERS, n_col)),
             dma((n_col,)),

time: 46.8 us -> 43.8 us (0.936)
  Pallas kernels: 43.9 us -> 40.9 us
    pallas_call x1, Pallas kernels: 43.9 us -> 40.9 us  [on_device(): pl.pallas_call(functools.partial(kernel, n_sub, n_col), out_shape=(out, o...]
where the time goes in v5:
time: 43.8 us; the launch traced here: 43.6 us
  Pallas kernels  40.9 us (93%)
  local copies, waits for them, and re-layouts  2 us (5%)
  between operations  0.65 us (1%)
    pallas_call x1, Pallas kernels, on_device(): pl.pallas_call(functools.partial(kernel, n_sub, n_col), out_shape=(out, o...  40.9 us
    unnamed x4, local copies, waits for them, and re-layouts  2 us

profile of v5, /device:TPU:0, one launch (start us, length us, event | category | flops | bytes accessed | tf_op | source)
XLA Modules:
  0.0 43.6 jit_solution(14560265712330116734)
XLA Ops:
  0.6 40.9 %feti_pcg.1 = (f32[1,1,4,2048]{3,2,1,0:T(4,128)}, f32[1,1,4,2048]{3,2,1,0:T(4,128)}) custom-call(f32[1,1,16,16,128]{4,3,2,1,0:T(8,128)} %loads_hbm.1, f32[1,1,16,16]{3,2,1,0:T(8,128)} %mode_x_hbm.1, f32[1,1,16,16]{3,2,1,0:T(8,128)} %mode_y_hbm.1, f32[1,1,128,128]{3,2,1,0:T(8,128)} %mode_z_hbm.1, f32[1,1,160]{2,1,0:T(1,128)} %eigen_hbm.1, ...), custom_call_target="tpu_custom_call" | custom-call | tf_op jit(solution)/shard_map/feti_pcg/pallas_call | solution.py:551
  41.5 0.0 copy-start
  41.6 1.4 %copy.16 = f32[1,1,4,2048]{3,2,1,0:T(4,128)} copy(f32[1,1,4,2048]{3,2,1,0:T(4,128)} %get-tuple-element.4) | data formatting | bytes 65536
  42.9 0.0 copy-done
  42.9 0.6 %copy.17 = f32[1,1,4,2048]{3,2,1,0:T(4,128)} copy(f32[1,1,4,2048]{3,2,1,0:T(4,128)S(1)} %copy-done) | data formatting | bytes 65536
Async XLA Ops:
  41.5 1.4 %copy-start = (f32[1,1,4,2048]{3,2,1,0:T(4,128)S(1)}, f32[1,1,4,2048]{3,2,1,0:T(4,128)}, u32[]{:S(2)}) copy-start(f32[1,1,4,2048]{3,2,1,0:T(4,128)} %get-tuple-element.5) | copy-start | bytes 98308

commit v6 on v5

--- a/solution.py
+++ b/solution.py
@@ -82,7 +82,6 @@
     placed_rows,
     node_z,
     node_p,
-    scaled,
     el_ref,
     pair_f,
     pair_b,
@@ -157,7 +156,7 @@
 
     def other(s):
         flat = lax.rem(own + s, n_all)
-        return flat // n_col, lax.rem(flat, n_col)
+        return lax.div(flat, n_col), lax.rem(flat, n_col)
 
     def greet_all(s):
         pl.semaphore_signal(barrier, inc=1, device_id=other(s), device_id_type=MESH)
@@ -418,32 +417,25 @@
         each(1, n_col, lambda s: col_copy(s).wait())
         return jnp.sum(vec_col[turn], axis=0)
 
-    def receive(turn):
+    def jump(turn, d):
+        copy_of(turn, d ^ 1).wait_recv()
+        return signs[d] * (send_v[turn, d] - recv_v[turn, d])
+
+    def scatter(value_of):
+        total = jnp.zeros((2 * size_z, plane), F32)
         for d in range(4):
-            copy_of(turn, d).wait()
-
-    def jump(turn):
-        receive(turn)
-        return [signs[d] * (send_v[turn, d] - recv_v[turn, d]) for d in range(4)]
-
-    def scatter(values):
-        for d in range(4):
-            scaled[d] = signs[d] * values[d]
-
-        def one(d, total):
-            high, low = halves(scaled[d])
+            high, low = halves(signs[d] * value_of(d))
             for at in range(0, width, CHUNK):
-                mask = masks[:, lanes(d, at)]
-                placed_rows[:size_z, at : at + CHUNK] = mask * high[:, at : at + CHUNK]
-                placed_rows[size_z:, at : at + CHUNK] = mask * low[:, at : at + CHUNK]
-            return total + lax.dot_general(
-                placed_rows[...],
-                onehot[:, pl.ds(pl.multiple_of(d * width, 128), width)],
+                here = slice(at, at + CHUNK)
+                mask = masks[:, d * width + at : d * width + at + CHUNK]
+                placed_rows[d, :size_z, here] = mask * high[:, here]
+                placed_rows[d, size_z:, here] = mask * low[:, here]
+            total = total + lax.dot_general(
+                placed_rows[d],
+                onehot[:, d * width : (d + 1) * width],
                 (((1,), (1,)), ((), ())),
                 preferred_element_type=F32,
             )
-
-        total = lax.fori_loop(0, 4, one, jnp.zeros((2 * size_z, plane), F32))
         return total[:size_z] + total[size_z:]
 
     def all_of(x):
@@ -457,8 +449,9 @@
 
     lane = iota((1, padded), 1)
 
-    def apply(turn, values, scalars):
-        modal = forward(scatter(values))
+    def apply(turn, value_of, scalars_of):
+        modal = forward(scatter(value_of))
+        scalars = scalars_of()
         spectral = lam_ref[...] * modal
         energy = all_of(modal * spectral)
         at_corner = jnp.sum(
@@ -492,23 +485,37 @@
         ]
         return 2.0 * (got[0] + quad), got[1:]
 
-    receive(0)
-    weight = []
-    for d in range(4):
+    four = range(4)
+    weight, resid, direction, image = [None] * 4, [None] * 4, [None] * 4, [None] * 4
+
+    def first_value(d):
+        copy_of(0, d ^ 1).wait_recv()
         near, far = send_v[0, d], recv_v[0, d]
-        weight.append(near * far / (near + far))
-    four = range(4)
-    resid = jump(1)
-    direction = [weight[d] * resid[d] for d in four]
-    image_dot, (rz,) = apply(2, direction, [dot4(resid, direction)])
+        weight[d] = near * far / (near + far)
+        resid[d] = jump(1, d)
+        direction[d] = weight[d] * resid[d]
+        return direction[d]
+
+    image_dot, (rz,) = apply(2, first_value, lambda: [dot4(resid, direction)])
     alpha = rz / image_dot
+    beta = None
     mult = [alpha * direction[d] for d in four]
-    image = jump(2)
+
+    def image_at(turn, d):
+        fresh = jump(turn, d)
+        return fresh if beta is None else fresh + beta * image[d]
+
     for step in range(1, ITERS):
-        resid = [resid[d] - alpha * image[d] for d in four]
-        precond = [weight[d] * resid[d] for d in four]
+        precond = [None] * 4
+
+        def next_value(d):
+            image[d] = image_at(1 + step, d)
+            resid[d] = resid[d] - alpha * image[d]
+            precond[d] = weight[d] * resid[d]
+            return precond[d]
+
         own_dot, (rz_next, cross) = apply(
-            2 + step, precond, [dot4(resid, precond), dot4(precond, image)]
+            2 + step, next_value, lambda: [dot4(resid, precond), dot4(precond, image)]
         )
         beta = rz_next / rz
         image_dot = own_dot + 2.0 * beta * cross + beta * beta * image_dot
@@ -516,8 +523,7 @@
         rz = rz_next
         direction = [precond[d] + beta * direction[d] for d in four]
         mult = [mult[d] + alpha * direction[d] for d in four]
-        fresh = jump(2 + step)
-        image = [fresh[d] + beta * image[d] for d in four]
+    image = [image_at(1 + ITERS, d) for d in four]
     resid = [resid[d] - alpha * image[d] for d in four]
     for k in range(4):
         share = [match[d][k].astype(F32) for d in four]
@@ -528,6 +534,9 @@
             two = two + share[d] * resid[d]
         out_mult[0, 0, k : k + 1, :] = one
         out_resid[0, 0, k : k + 1, :] = two
+    for turn in range(2 + ITERS):
+        for d in four:
+            copy_of(turn, d).wait_send()
 
 
 def on_device(n_sub, n_col, *args):
@@ -561,10 +570,9 @@
             dma((8,)),
             pltpu.VMEM((plane, 4 * width), BF),
             pltpu.VMEM((size_z, 4 * width), BF),
-            pltpu.VMEM((2 * size_z, width), BF),
+            pltpu.VMEM((4, 2 * size_z, width), BF),
             pltpu.VMEM((4, 1, width), jnp.int32),
             pltpu.VMEM((4, 1, width), jnp.int32),
-            pltpu.VMEM((4, 1, width), F32),
             pltpu.VMEM((128, 128), F32),
             pltpu.VMEM((3 * plane, plane), BF),
             pltpu.VMEM((3 * plane, plane), BF),

time: 43.8 us -> 43.3 us (0.989)
  Pallas kernels: 40.9 us -> 40.4 us
    pallas_call x1, Pallas kernels: 40.9 us -> 40.4 us  [on_device(): pl.pallas_call(functools.partial(kernel, n_sub, n_col), out_shape=(out, o...]
where the time goes in v6:
time: 43.3 us; the launch traced here: 43.1 us
  Pallas kernels  40.4 us (93%)
  local copies, waits for them, and re-layouts  2 us (5%)
  between operations  0.65 us (2%)
    pallas_call x1, Pallas kernels, on_device(): pl.pallas_call(functools.partial(kernel, n_sub, n_col), out_shape=(out, o...  40.4 us
    unnamed x4, local copies, waits for them, and re-layouts  2 us

profile of v6, /device:TPU:0, one launch (start us, length us, event | category | flops | bytes accessed | tf_op | source)
XLA Modules:
  0.0 43.1 jit_solution(13548585890148846467)
XLA Ops:
  0.6 40.4 %feti_pcg.1 = (f32[1,1,4,2048]{3,2,1,0:T(4,128)}, f32[1,1,4,2048]{3,2,1,0:T(4,128)}) custom-call(f32[1,1,16,16,128]{4,3,2,1,0:T(8,128)} %loads_hbm.1, f32[1,1,16,16]{3,2,1,0:T(8,128)} %mode_x_hbm.1, f32[1,1,16,16]{3,2,1,0:T(8,128)} %mode_y_hbm.1, f32[1,1,128,128]{3,2,1,0:T(8,128)} %mode_z_hbm.1, f32[1,1,160]{2,1,0:T(1,128)} %eigen_hbm.1, ...), custom_call_target="tpu_custom_call" | custom-call | tf_op jit(solution)/shard_map/feti_pcg/pallas_call | solution.py:560
  41.1 0.0 copy-start
  41.1 1.4 %copy.16 = f32[1,1,4,2048]{3,2,1,0:T(4,128)} copy(f32[1,1,4,2048]{3,2,1,0:T(4,128)} %get-tuple-element.4) | data formatting | bytes 65536
  42.5 0.0 copy-done
  42.5 0.6 %copy.17 = f32[1,1,4,2048]{3,2,1,0:T(4,128)} copy(f32[1,1,4,2048]{3,2,1,0:T(4,128)S(1)} %copy-done) | data formatting | bytes 65536
Async XLA Ops:
  41.1 1.4 %copy-start = (f32[1,1,4,2048]{3,2,1,0:T(4,128)S(1)}, f32[1,1,4,2048]{3,2,1,0:T(4,128)}, u32[]{:S(2)}) copy-start(f32[1,1,4,2048]{3,2,1,0:T(4,128)} %get-tuple-element.5) | copy-start | bytes 98308

commit v7 on v6

--- a/solution.py
+++ b/solution.py
@@ -8,7 +8,7 @@
 from jax.sharding import PartitionSpec as P
 
 ITERS = 2
-CHUNK = 512
+CHUNK = 256
 DIRECT = 64
 BF = jnp.bfloat16
 F32 = jnp.float32

time: 43.3 us -> 43.5 us (level)
  no operation moved by 1% of the time
where the time goes in v7:
time: 43.5 us; the launch traced here: 43.3 us
  Pallas kernels  40.7 us (94%)
  local copies, waits for them, and re-layouts  2 us (5%)
  between operations  0.65 us (1%)
    pallas_call x1, Pallas kernels, on_device(): pl.pallas_call(functools.partial(kernel, n_sub, n_col), out_shape=(out, o...  40.7 us
    unnamed x4, local copies, waits for them, and re-layouts  2 us

profile of v7, /device:TPU:0, one launch (start us, length us, event | category | flops | bytes accessed | tf_op | source)
XLA Modules:
  0.0 43.3 jit_solution(14764139229256490201)
XLA Ops:
  0.6 40.7 %feti_pcg.1 = (f32[1,1,4,2048]{3,2,1,0:T(4,128)}, f32[1,1,4,2048]{3,2,1,0:T(4,128)}) custom-call(f32[1,1,16,16,128]{4,3,2,1,0:T(8,128)} %loads_hbm.1, f32[1,1,16,16]{3,2,1,0:T(8,128)} %mode_x_hbm.1, f32[1,1,16,16]{3,2,1,0:T(8,128)} %mode_y_hbm.1, f32[1,1,128,128]{3,2,1,0:T(8,128)} %mode_z_hbm.1, f32[1,1,160]{2,1,0:T(1,128)} %eigen_hbm.1, ...), custom_call_target="tpu_custom_call" | custom-call | tf_op jit(solution)/shard_map/feti_pcg/pallas_call | solution.py:560
  41.3 0.0 copy-start
  41.3 1.4 %copy.16 = f32[1,1,4,2048]{3,2,1,0:T(4,128)} copy(f32[1,1,4,2048]{3,2,1,0:T(4,128)} %get-tuple-element.4) | data formatting | bytes 65536
  42.7 0.0 copy-done
  42.7 0.6 %copy.17 = f32[1,1,4,2048]{3,2,1,0:T(4,128)} copy(f32[1,1,4,2048]{3,2,1,0:T(4,128)S(1)} %copy-done) | data formatting | bytes 65536
Async XLA Ops:
  41.3 1.4 %copy-start = (f32[1,1,4,2048]{3,2,1,0:T(4,128)S(1)}, f32[1,1,4,2048]{3,2,1,0:T(4,128)}, u32[]{:S(2)}) copy-start(f32[1,1,4,2048]{3,2,1,0:T(4,128)} %get-tuple-element.5) | copy-start | bytes 98308
